TPU v7x, 512 devices: a whole 4x4x16 slice. The times are simulated.
512 devices in a mesh: cols: 128 (over z, x, core), rep: 4 (over y).
Axes of the slice: x: 4, y: 4, z: 16, core: 2. Of those that a mesh axis runs over, the one named last changes fastest.
Arguments:
- features: bfloat16 [65536, 768], P(None, 'cols'), may hold values from -6 to 6
- self_ids: int32 [128, 32], P(None, 'rep'), may hold values from 0 to 65535
- nbr_ids: int32 [128, 32, 25], P(None, 'rep'), may hold values from 0 to 65535
- nbr_counts: int32 [128, 32], P(None, 'rep'), may hold values from 1 to 25
- w1_self: bfloat16 [768, 1024], P('cols'), may hold values from -0.21875 to 0.21875
- w1_nbr: bfloat16 [768, 1024], P('cols'), may hold values from -0.21875 to 0.21875
- bias1: float32 [1024], replicated, may hold values from -4 to 4
- w2_self: bfloat16 [1024, 153], replicated, may hold values from -0.25 to 0.25
- w2_nbr: bfloat16 [1024, 153], replicated, may hold values from -0.25 to 0.25
- bias2: float32 [153], replicated, may hold values from -4 to 4
- labels: int32 [4096], P(('cols', 'rep')), may hold values from 0 to 152, as said below
- top_ids: int32 [4096, 15], P(('cols', 'rep')), may hold values from 0 to 7
- top_counts: int32 [4096], P(('cols', 'rep')), may hold values from 1 to 15
Outputs:
- loss: float32 [], replicated
- grad_w1_self: float32 [768, 1024], P('cols')
- grad_w1_nbr: float32 [768, 1024], P('cols')
- grad_bias1: float32 [1024], replicated
- grad_w2_self: float32 [1024, 153], replicated
- grad_w2_nbr: float32 [1024, 153], replicated
- grad_bias2: float32 [153], replicated
Inputs may be any that keep to these rules, and one draw needn't show every extreme that they name: `nbr_counts`: entries beyond a row's count are padding. `top_counts`: entries beyond a row's count are padding. `labels`: in each aligned block of 8 rows, the first 4 rows share one class; the others are drawn independently.
All inputs are finite; a program needn't handle non-finite values.
Results may differ from a plain program's by a relative error of at most 0.0037.
The roundings to bfloat16 on the way count: a program that leaves them out, or rounds other values in their place, can miss the bound.
Values may be sent and summed in bfloat16 or wider, within the bound.
A program may use at most 128 MiB of HBM per device.

v0:
```python
import jax
import jax.numpy as jnp
from jax import lax
from jax.sharding import PartitionSpec as P

loss_scale = 64.0


def contract_rows(left, right):
    return lax.dot_general(
        left, right, (((0,), (0,)), ((), ())), preferred_element_type=jnp.float32
    )


def contract_cols(left, right):
    return lax.dot_general(
        left, right, (((1,), (1,)), ((), ())), preferred_element_type=jnp.float32
    )


def per_device(
    features,
    self_ids,
    nbr_ids,
    nbr_counts,
    w1_self,
    w1_nbr,
    bias1,
    w2_self,
    w2_nbr,
    bias2,
    labels,
    top_ids,
    top_counts,
):
    owners, rows_own = self_ids.shape
    group_rows = owners * rows_own
    fanout = nbr_ids.shape[2]
    col_width = features.shape[1]
    classes = w2_self.shape[1]
    targets = rows_own * lax.axis_size("cols") * lax.axis_size("rep")
    selfin = jnp.take(features, self_ids.reshape(group_rows), axis=0)
    picked = (
        jnp.take(features, nbr_ids.reshape(group_rows * fanout), axis=0)
        .reshape(group_rows, fanout, col_width)
        .astype(jnp.float32)
    )
    is_live = lax.broadcasted_iota(jnp.int32, (group_rows, fanout), 1) < nbr_counts.reshape(
        group_rows, 1
    )
    summed = jnp.sum(jnp.where(is_live[:, :, None], picked, jnp.float32(0.0)), axis=1)
    nbrmean = (summed / nbr_counts.reshape(group_rows, 1).astype(jnp.float32)).astype(jnp.bfloat16)
    rows_self = selfin
    rows_nbr = nbrmean
    layer_sum = lax.psum_scatter(
        jnp.dot(rows_self, w1_self, preferred_element_type=jnp.float32)
        + jnp.dot(rows_nbr, w1_nbr, preferred_element_type=jnp.float32),
        "cols",
        scatter_dimension=0,
        tiled=True,
    )
    pre_act = layer_sum + bias1
    hidden = jnp.maximum(pre_act, 0.0).astype(jnp.bfloat16)
    fan_top = top_ids.shape[1]
    top_live = lax.broadcasted_iota(jnp.int32, (rows_own, fan_top), 1) < top_counts[:, None]
    slots = lax.broadcasted_iota(jnp.int32, (1, 1, rows_own), 2)
    counts_matrix = jnp.sum(
        jnp.where(
            top_live[:, :, None] & (top_ids[:, :, None] == slots),
            jnp.float32(1.0),
            jnp.float32(0.0),
        ),
        axis=1,
    )
    top_div = top_counts.astype(jnp.float32)[:, None]
    top_sum = jnp.dot(
        counts_matrix.astype(jnp.bfloat16), hidden, preferred_element_type=jnp.float32
    )
    top_mean = (top_sum / top_div).astype(jnp.bfloat16)
    logits = (
        jnp.dot(hidden, w2_self, preferred_element_type=jnp.float32)
        + jnp.dot(top_mean, w2_nbr, preferred_element_type=jnp.float32)
        + bias2
    )
    exps = jnp.exp(logits)
    total = jnp.sum(exps, axis=1)
    onehot = jnp.where(
        lax.broadcasted_iota(jnp.int32, (rows_own, classes), 1) == labels[:, None],
        jnp.float32(1.0),
        jnp.float32(0.0),
    )
    row_loss = jnp.log(total) - jnp.sum(onehot * logits, axis=1)
    grad_logits = ((exps / total[:, None] - onehot) * (loss_scale / targets)).astype(jnp.bfloat16)
    local_w2_self = contract_rows(hidden, grad_logits)
    local_w2_nbr = contract_rows(top_mean, grad_logits)
    local_bias2 = jnp.sum(grad_logits.astype(jnp.float32), axis=0)
    back_self = contract_cols(grad_logits, w2_self)
    back_top = contract_cols(grad_logits, w2_nbr) / top_div
    back_hidden = back_self + jnp.dot(counts_matrix.T, back_top, precision=lax.Precision.HIGHEST)
    grad_pre = jnp.where(pre_act > 0.0, back_hidden, jnp.float32(0.0)).astype(jnp.bfloat16)
    local_bias1 = jnp.sum(grad_pre.astype(jnp.float32), axis=0)
    loss_sum, grad_w2_self, grad_w2_nbr, grad_bias2, grad_bias1 = lax.psum(
        (jnp.sum(row_loss), local_w2_self, local_w2_nbr, local_bias2, local_bias1), ("cols", "rep")
    )
    pieces = lax.all_gather(grad_pre, "cols", axis=0, tiled=True)
    rows_self = selfin
    rows_nbr = nbrmean
    part_self = contract_rows(rows_self, pieces)
    part_nbr = contract_rows(rows_nbr, pieces)
    grad_w1_self, grad_w1_nbr = lax.psum((part_self, part_nbr), "rep")
    loss = loss_sum / targets
    return (loss, grad_w1_self, grad_w1_nbr, grad_bias1, grad_w2_self, grad_w2_nbr, grad_bias2)


def solution(mesh):
    in_specs = (
        P(None, "cols"),
        P(None, "rep"),
        P(None, "rep", None),
        P(None, "rep"),
        P("cols", None),
        P("cols", None),
        P(),
        P(),
        P(),
        P(),
        P(("cols", "rep")),
        P(("cols", "rep"), None),
        P(("cols", "rep")),
    )
    out_specs = (P(), P("cols", None), P("cols", None), P(), P(), P(), P())
    return jax.shard_map(
        per_device, mesh=mesh, in_specs=in_specs, out_specs=out_specs, check_vma=False
    )
```

profile of v0, /device:TPU:1, one launch (start us, length us, event | category | flops | bytes accessed | tf_op | source)
XLA Modules:
  0.0 1034.4 jit_solution(15457752920657667840)
XLA Ops:
  7.2 0.0 copy-start
  7.2 0.0 copy-start.2
  7.2 0.0 reduce-scatter.2.cloned.1.call-start
  7.2 0.9 copy.38
  8.1 0.1 reshape.156
  8.2 0.1 reshape.155
  8.3 0.8 copy.41
  9.1 0.1 lt.73
  9.2 1.1 copy.42
  10.3 0.4 reshape.158
  10.8 0.3 iota_compare_fusion
  11.2 0.1 compare_select_fusion.1
  11.3 0.0 copy-done.2
  11.3 11.3 %copy.40 = bf16[65536,6]{1,0:T(8,128)(2,1)} copy(bf16[65536,6]{0,1:T(8,128)(2,1)S(1)} %copy-done.2) | data formatting | bytes 1572864 | tf_op args[0]
  22.6 10.8 %gather_fusion = bf16[1024,6]{1,0:T(8,128)(2,1)S(1)} fusion(bf16[65536,6]{1,0:T(8,128)(2,1)} %copy.40, s32[1024]{0:T(1024)S(1)} %broadcast_clamp_fusion.1), kind=kCustom, calls=%fused_computation | custom fusion | bytes 28672 | tf_op jit(solution)/shard_map/jit(_take)/gather | solution.py:42
  33.4 93.4 %gather_fusion.1 = bf16[25600,6]{1,0:T(8,128)(2,1)} fusion(bf16[65536,6]{1,0:T(8,128)(2,1)} %copy.40, s32[25600]{0:T(1024)S(1)} %broadcast_clamp_fusion), kind=kCustom, calls=%fused_computation.1 | custom fusion | bytes 716800 | tf_op jit(solution)/shard_map/jit(_take)/gather | solution.py:44
  126.8 5.4 copy.45
  132.1 0.0 copy-start.3
  132.2 3.6 gather.12
  135.8 0.0 copy-start.4
  135.8 1.4 select_reduce_fusion
  137.2 0.0 copy-done.3
  137.2 0.8 fusion.5
  138.0 0.0 copy-done.4
  138.0 2.7 convolution_add_fusion
  140.7 0.0 copy-start.6
  140.7 0.0 copy-start.5
  140.7 0.0 copy-start.1
  140.7 0.0 copy-start.7
  140.7 0.0 copy-start.8
  140.7 0.0 reduce-scatter.2.cloned.1.call-update
  140.7 0.2 all-gather.2.cloned.1.call-start
  141.0 0.4 copy-done.9
  141.3 0.1 iota_compare_fusion.3
  141.4 0.0 copy-done.6
  141.4 0.1 select_reduce_fusion.1
  141.5 258.0 %reduce-scatter.2.cloned.1.call-done = f32[8,1024]{1,0:T(8,128)} async-done(((f32[1024,1024]{1,0:T(8,128)}), f32[8,1024]{1,0:T(8,128)}) %reduce-scatter.2.cloned.1.call-update) | async-done | bytes 32784 | tf_op jit(solution)/shard_map/reduce_scatter | solution.py:55
  399.5 0.0 copy-done.5
  399.5 0.8 maximum_convert_fusion
  400.3 0.0 copy-done.1
  400.3 0.2 fusion.15
  400.5 0.1 fusion.1
  400.6 0.0 copy-done
  400.6 0.0 copy-done.7
  400.6 0.0 copy-done.8
  400.6 0.3 exponential_reduce_fusion
  400.9 0.1 convert_reduce_fusion.1
  401.0 0.2 convolution_divide_fusion
  401.2 0.2 fusion.16
  401.4 1.6 convert_reduce_fusion
  403.0 0.0 all-gather.2.cloned.1.call-update
  403.0 0.0 all-reduce.5.cloned.1.call-start
  403.0 1.1 fusion.18
  404.2 1.1 fusion.17
  405.3 0.0 all-reduce.5.cloned.1.call-update
  405.3 0.6 subtract_reduce_fusion
  405.9 113.2 %all-reduce = (f32[]{:T(128)}, f32[1024]{0:T(1024)}, f32[153]{0:T(256)}) all-reduce(f32[]{:T(128)} %subtract_reduce_fusion, f32[1024]{0:T(1024)S(1)} %get-tuple-element.19, f32[153]{0:T(256)S(1)} %get-tuple-element.16), channel_id=1, replica_groups=mesh['cols'=128,'rep'=4] {'cols','rep'}, use_global_device_ids=true, to_apply=%region_6.7 | all-reduce | flops 1178 | bytes 9424 | tf_op jit(solution)/shard_map/psum | solution.py:102
  519.8 32.5 %all-gather.2.cloned.1.call-done = bf16[1024,1024]{1,0:T(8,128)(2,1)} async-done(((bf16[8,1024]{1,0:T(8,128)(2,1)}), bf16[1024,1024]{1,0:T(8,128)(2,1)}) %all-gather.2.cloned.1.call-update) | async-done | bytes 2097168 | tf_op jit(solution)/shard_map/all_gather | solution.py:105
  552.3 2.0 fusion.13
  554.3 2.2 fusion.4
  556.4 14.3 %all-reduce.2 = (f32[6,1024]{1,0:T(8,128)}, f32[6,1024]{1,0:T(8,128)}) all-reduce(f32[6,1024]{1,0:T(8,128)S(1)} %fusion.4, f32[6,1024]{1,0:T(8,128)S(1)} %fusion.13), channel_id=1, replica_groups=mesh['cols'=128,'rep'=4] {'rep'}, use_global_device_ids=true, to_apply=%region_7.8 | all-reduce | flops 12288 | bytes 98304 | tf_op jit(solution)/shard_map/psum | solution.py:110
  570.7 452.0 %all-reduce.5.cloned.1.call-done = (f32[1024,153]{0,1:T(8,128)}, f32[1024,153]{0,1:T(8,128)}) async-done(((f32[1024,153]{0,1:T(8,128)}, f32[1024,153]{0,1:T(8,128)}), (f32[1024,153]{0,1:T(8,128)}, f32[1024,153]{0,1:T(8,128)})) %all-reduce.5.cloned.1.call-update) | async-done | bytes 1253392 | tf_op jit(solution)/shard_map/psum | solution.py:102
  1022.7 2.0 copy.48
  1024.7 2.0 copy.49
  (7 shorter events, 0.0 us)
Async XLA Ops:
  7.2 393.4 %copy-start = (bf16[1024,153]{0,1:T(8,128)(2,1)S(1)}, bf16[1024,153]{0,1:T(8,128)(2,1)}, u32[]{:S(2)}) copy-start(bf16[1024,153]{0,1:T(8,128)(2,1)} %param.21) | copy-start | bytes 940036
  7.2 4.1 copy-start.2
  7.2 392.3 %reduce-scatter.2.cloned.1.call-start = ((), (), s32[]{:S(2)}) async-start(), calls=%async_computation.1 | async-start | bytes 4227072 | tf_op jit(solution)/shard_map/reduce_scatter | solution.py:55
  132.1 5.1 copy-start.3
  135.8 2.2 copy-start.4
  140.7 0.7 copy-start.9
  140.7 0.7 copy-start.6
  140.7 258.8 %copy-start.5 = (f32[1024]{0:T(1024)S(1)}, f32[1024]{0:T(1024)}, u32[]{:S(2)}) copy-start(f32[1024]{0:T(1024)} %param.19) | copy-start | bytes 12292
  140.7 259.6 %copy-start.1 = (bf16[1024,153]{0,1:T(8,128)(2,1)S(1)}, bf16[1024,153]{0,1:T(8,128)(2,1)}, u32[]{:S(2)}) copy-start(bf16[1024,153]{0,1:T(8,128)(2,1)} %param.20) | copy-start | bytes 940036
  140.7 259.9 %copy-start.7 = (s32[8]{0:T(128)S(1)}, s32[8]{0:T(128)}, u32[]{:S(2)}) copy-start(s32[8]{0:T(128)} %param.23) | copy-start | bytes 100
  140.7 259.9 %copy-start.8 = (f32[153]{0:T(256)S(1)}, f32[153]{0:T(256)}, u32[]{:S(2)}) copy-start(f32[153]{0:T(256)} %param.22) | copy-start | bytes 1840
  140.7 411.6 %all-gather.2.cloned.1.call-start = ((), (), s32[]{:S(2)}) async-start(), calls=%async_computation.2 | async-start | bytes 2113536 | tf_op jit(solution)/shard_map/all_gather | solution.py:105
  403.0 619.8 %all-reduce.5.cloned.1.call-start = ((), (), s32[]{:S(2)}) async-start(), calls=%async_computation.3 | async-start | bytes 2621440 | tf_op jit(solution)/shard_map/psum | solution.py:102
Sparse Core Ops, SparseCore 0:
  140.9 258.6 reduce-scatter.1
  403.2 149.0 all-gather.1
  558.4 464.3 all-reduce.4
where the time goes:
time: 1030 us
  waiting for transfers between devices  743 us (72%)
  local copies, waits for them, and re-layouts  132 us (13%)
  blocking collectives  127 us (12%)
  between operations  15.7 us (2%)
  matrix products  12.4 us (1%)
    psum x1, waiting for transfers between devices, per_device(): lax.psum((jnp.sum(row_loss), local_w2_self, local_w2_nbr, local_bias2, lo...  452 us
    reduce_scatter x1, waiting for transfers between devices, per_device(): lax.psum_scatter(jnp.dot(rows_self, w1_self, preferred_element_type=jnp.f...  258 us
    psum x1, blocking collectives, per_device(): lax.psum((jnp.sum(row_loss), local_w2_self, local_w2_nbr, local_bias2, lo...  113 us
    gather x3, local copies, waits for them, and re-layouts, per_device(): jnp.take(features, nbr_ids.reshape(group_rows * fanout), axis=0)  102 us
    all_gather x1, waiting for transfers between devices, per_device(): pieces = lax.all_gather(grad_pre, 'cols', axis=0, tiled=True)  32.5 us
  transfers between devices with their start and end apart: 3, of which 3 were waited for; matrix products, arithmetic and copies ran while one was open for 1% of the time, Pallas kernels for 0%

commit v1 on v0

v1 whole, which is shorter than its diff:
```python
import jax
import jax.numpy as jnp
from jax import lax
from jax.experimental import pallas as pl
from jax.experimental.pallas import tpu as pltpu
from jax.sharding import PartitionSpec as P

f32, bf16 = jnp.float32, jnp.bfloat16
loss_scale = 64.0

NZ, NG, NY, NX = 16, 8, 4, 4
LOW = 512
HIGH = 65536 // LOW
COLS = 6
FAN = 25
CLASSES = 153
LOSS_LANE = 200
FIN_ROWS = 24
SPAN = 128
VMEM = pltpu.VMEM

SEMS = {}
total_sems = 0
for stage, slots in (
    ("w_g", NG), ("aux", NG), ("w_z", NZ), ("x_z", NZ), ("x_g", NG), ("xg", NG), ("lr", NG), ("gl", NG),
    ("gp", NZ), ("rs", NZ), ("y1", NY), ("fz", NZ), ("fx", NX), ("fc", 2), ("dw", NG), ("y2", NY),
):
    SEMS[stage] = total_sems
    total_sems += slots


def dot(a, b, ca=1, cb=0):
    return lax.dot_general(a, b, (((ca,), (cb,)), ((), ())), preferred_element_type=f32)


def iota(shape, dim):
    return lax.broadcasted_iota(jnp.int32, shape, dim)


def step_kernel(
    feat, self_ids, nbr_ids, nbr_counts, w1s, w1n, bias1, w2s, w2n, bias2, labels, top_ids, top_counts,
    loss_out, g1s_out, g1n_out, gb1_out, g2s_out, g2n_out, gb2_out,
    split, table, wt, w_src, w_mid, w_all, aux, rows_t, rows_m, xp, x_src, x_in, x_mid, x_all, xg,
    lp, lr, gl_src, gl_all, gp_src, gp_all, g2, rs, y1, full, dw_src, dw_in, y2, send_sem, recv_sem,
):
    o = lax.axis_index("cols")
    y = lax.axis_index("rep")
    z = o // NG
    g = o % NG
    x = g // 2
    c = g % 2

    def to_z(p):
        return {"cols": ((z + p) % NZ) * NG + g, "rep": y}

    def to_g(p):
        return {"cols": z * NG + (g + p) % NG, "rep": y}

    def to_y(p):
        return {"cols": o, "rep": (y + p) % NY}

    def to_x(p):
        return {"cols": z * NG + ((x + p) % NX) * 2 + c, "rep": y}

    def copy(stage, p, src, dst, device):
        at = SEMS[stage] + p
        return pltpu.make_async_remote_copy(
            src_ref=src, dst_ref=dst, send_sem=send_sem.at[at], recv_sem=recv_sem.at[at], device_id=device
        )

    def each(n, body):
        def run(p, carry):
            body(p)
            return carry
        lax.fori_loop(1, n, run, 0)

    barrier = pltpu.get_barrier_semaphore()
    each(NZ, lambda p: pl.semaphore_signal(barrier, inc=1, device_id=to_z(p)))
    each(NG, lambda p: pl.semaphore_signal(barrier, inc=1, device_id=to_g(p)))
    each(NY, lambda p: pl.semaphore_signal(barrier, inc=1, device_id=to_y(p)))

    wt[...] = jnp.zeros_like(wt)
    wt[0:COLS, :] = w1s[...].astype(f32)
    wt[COLS:2 * COLS, :] = w1n[...].astype(f32)
    for d in range(NG):
        w_src[d] = wt[:, d * SPAN:(d + 1) * SPAN].astype(bf16)
    w_mid[g] = w_src[g]

    eye = iota((8, 8), 0) == iota((8, 8), 1)

    def column(ref):
        return jnp.sum(jnp.where(eye, jnp.broadcast_to(ref[...].astype(f32), (8, 8)), 0.0), axis=1, keepdims=True)

    count_col = column(top_counts)
    label_col = column(labels)
    picks = top_ids[...]
    live_top = iota(picks.shape, 1).astype(f32) < count_col
    lane = iota((8, SPAN), 1)
    mine = jnp.where(lane == 8, count_col, jnp.where(lane == 9, label_col, 0.0))
    for s in range(8):
        n_s = jnp.sum(jnp.where(live_top & (picks == s), 1.0, 0.0), axis=1, keepdims=True)
        mine = jnp.where(lane == s, n_s, mine)
    aux[g] = mine

    pl.semaphore_wait(barrier, NZ + NG + NY - 3)

    each(NG, lambda p: copy("w_g", p, w_src.at[(g + p) % NG], w_mid.at[g], to_g(p)).start())
    each(NG, lambda p: copy("aux", p, aux.at[g], aux.at[g], to_g(p)).start())

    def split_high(h, carry):
        piece = feat[:, pl.ds(pl.multiple_of(h * LOW, LOW), LOW)].astype(f32)
        for q in range(LOW // SPAN):
            split[q, pl.ds(pl.multiple_of(h * 8, 8), COLS), :] = piece[:, q * SPAN:(q + 1) * SPAN]
        return carry

    lax.fori_loop(0, HIGH, split_high, 0, unroll=8)
    for k in range(COLS):
        for q in range(LOW // SPAN):
            table[k * HIGH:(k + 1) * HIGH, q * SPAN:(q + 1) * SPAN] = split[q, pl.ds(k, HIGH, stride=8), :].astype(bf16)

    each(NG, lambda p: copy("w_g", p, w_src.at[(g + p) % NG], w_mid.at[(g + NG - p) % NG], to_g(p)).wait_recv())
    w_all[z] = w_mid[...].reshape(SPAN, SPAN)
    each(NZ, lambda p: copy("w_z", p, w_all.at[z], w_all.at[z], to_z(p)).start())

    io_low = iota((LOW, SPAN), 0)
    io_high = iota((HIGH, SPAN), 0)
    counts = nbr_counts[...]

    def look(ids, alive):
        low = jnp.bitwise_and(ids, LOW - 1)
        high = jnp.where(alive, jnp.right_shift(ids, LOW.bit_length() - 1), -1)
        hot = jnp.concatenate([(io_low == low[j:j + 1, :]).astype(f32).astype(bf16) for j in range(8)], axis=1)
        mask = jnp.concatenate([io_high == high[j:j + 1, :] for j in range(8)], axis=1)
        got = dot(table[...], hot)
        return tuple(
            jnp.sum(jnp.where(mask, got[k * HIGH:(k + 1) * HIGH], 0.0).reshape(HIGH // 8, 8, 8 * SPAN), axis=0)
            for k in range(COLS)
        )

    own = look(self_ids[...], counts > 0)

    def add_nbr(k, sums):
        return tuple(a + b for a, b in zip(sums, look(nbr_ids[k], counts > k)))

    sums = lax.fori_loop(0, FAN, add_nbr, tuple(jnp.zeros((8, 8 * SPAN), f32) for _ in range(COLS)))
    rows_t[...] = jnp.zeros_like(rows_t)
    for j in range(8):
        cut = slice(j * SPAN, (j + 1) * SPAN)
        count = counts[j:j + 1, :].astype(f32)
        for k in range(COLS):
            rows_t[j, k:k + 1, :] = jnp.sum(own[k][:, cut], axis=0, keepdims=True)
            rows_t[j, COLS + k:COLS + k + 1, :] = jnp.sum(sums[k][:, cut], axis=0, keepdims=True) / count
    for j in range(8):
        rows_m[pl.ds(j, SPAN, stride=8), :] = rows_t[j].T
    for t in range(8):
        xp[t] = rows_m[t * SPAN:(t + 1) * SPAN, :].T[0:16, :].astype(bf16)

    odd = z % 2
    half = iota((16, SPAN), 1) // 64
    for t in range(8):
        straight = xp[t].astype(f32)
        turned = pltpu.roll(straight, 64, 1)
        x_src[2 * t] = jnp.where(half == odd, jnp.where(odd == 0, straight, turned), 0.0).astype(bf16)
        x_src[2 * t + 1] = jnp.where(half == odd, jnp.where(odd == 1, straight, turned), 0.0).astype(bf16)
    each(NZ, lambda p: copy("x_z", p, x_src.at[(z + p) % NZ], x_in.at[z], to_z(p)).start())
    x_in[z] = x_src[z]
    xg[g] = xp[...]
    each(NZ, lambda p: copy("x_z", p, x_src.at[(z + p) % NZ], x_in.at[(z + NZ - p) % NZ], to_z(p)).wait_recv())
    for t in range(8):
        x_mid[t] = x_in[2 * t] + x_in[2 * t + 1]
    each(NG, lambda p: copy("x_g", p, x_mid, x_all.at[g], to_g(p)).start())
    each(NG, lambda p: copy("xg", p, xp, xg.at[g], to_g(p)).start())
    x_all[g] = x_mid[...]

    each(NG, lambda p: copy("aux", p, aux.at[g], aux.at[(g + NG - p) % NG], to_g(p)).wait_recv())
    lists = aux[...].reshape(64, SPAN)
    top_div = lists[:, 8:9]
    spread = (iota((SPAN, 64), 0) == iota((SPAN, 64), 1) % 8).astype(f32).astype(bf16)
    same = iota((64, 64), 0) // 8 == iota((64, 64), 1) // 8
    picked = jnp.where(same, dot(lists.astype(bf16), spread), 0.0).astype(bf16)

    each(NZ, lambda p: copy("w_z", p, w_all.at[z], w_all.at[(z + NZ - p) % NZ], to_z(p)).wait_recv())
    each(NG, lambda p: copy("x_g", p, x_mid, x_all.at[(g + NG - p) % NG], to_g(p)).wait_recv())

    both = jnp.zeros((SPAN, 2 * SPAN), f32)
    for t in range(8):
        left = x_all[:, t].reshape(SPAN, SPAN)
        right = jnp.concatenate([w_all[2 * t], w_all[2 * t + 1]], axis=1)
        both = both + dot(left, right, 0, 0)
    pre = both[0:64, 0:SPAN] + both[64:SPAN, SPAN:] + bias1[pl.ds(g, 1), :]
    hidden = jnp.maximum(pre, 0.0).astype(bf16)
    top_mean = (dot(picked, hidden) / top_div).astype(bf16)
    span = pl.ds(pl.multiple_of(g * SPAN, SPAN), SPAN)
    w2s_g = w2s[:, span]
    w2n_g = w2n[:, span]
    part = dot(hidden, w2s_g, 1, 1) + dot(top_mean, w2n_g, 1, 1)
    lp[...] = jnp.zeros_like(lp)
    lp[:, :, 0:CLASSES] = part.reshape(NG, 8, CLASSES)
    each(NG, lambda p: copy("lr", p, lp.at[(g + p) % NG], lr.at[g], to_g(p)).start())
    lr[g] = lp[g]
    each(NG, lambda p: copy("lr", p, lp.at[(g + p) % NG], lr.at[(g + NG - p) % NG], to_g(p)).wait_recv())

    logits = jnp.sum(lr[...], axis=0)[:, 0:CLASSES] + bias2[...]
    exps = jnp.exp(logits)
    total = jnp.sum(exps, axis=1, keepdims=True)
    onehot = jnp.where(iota((8, CLASSES), 1).astype(f32) == label_col, 1.0, 0.0)
    row_loss = jnp.log(total) - jnp.sum(onehot * logits, axis=1, keepdims=True)
    targets = 8 * NG * NZ * NY
    grad = ((exps / total - onehot) * (loss_scale / targets)).astype(bf16)
    gl_src[...] = jnp.where(iota((8, 2 * SPAN), 1) == LOSS_LANE, row_loss, 0.0)
    gl_src[:, 0:CLASSES] = grad.astype(f32)
    each(NG, lambda p: copy("gl", p, gl_src, gl_all.at[g], to_g(p)).start())
    gl_all[g] = gl_src[...]
    each(NG, lambda p: copy("gl", p, gl_src, gl_all.at[(g + NG - p) % NG], to_g(p)).wait_recv())

    gl_rows = gl_all[...].reshape(64, 2 * SPAN)
    gl = gl_rows[:, 0:CLASSES].astype(bf16)
    back_top = dot(gl, w2n_g) / top_div
    top_1 = back_top.astype(bf16)
    rest = back_top - top_1.astype(f32)
    top_2 = rest.astype(bf16)
    top_3 = (rest - top_2.astype(f32)).astype(bf16)
    back = dot(gl, w2s_g) + (dot(picked, top_1, 0, 0) + (dot(picked, top_2, 0, 0) + dot(picked, top_3, 0, 0)))
    grad_pre = jnp.where(pre > 0.0, back, 0.0).astype(bf16)
    gp_src[...] = grad_pre
    each(NZ, lambda p: copy("gp", p, gp_src, gp_all.at[z], to_z(p)).start())
    gp_all[z] = gp_src[...]

    g2[...] = jnp.zeros_like(g2)
    g2[0:CLASSES, :] = dot(gl, hidden, 0, 0)
    g2[160:160 + CLASSES, :] = dot(gl, top_mean, 0, 0)
    g2[320:321, :] = jnp.sum(grad_pre.astype(f32), axis=0, keepdims=True)
    col_sums = jnp.sum(gl_rows, axis=0, keepdims=True)
    g2[321:322, :] = col_sums[:, 0:SPAN]
    g2[322:323, :] = col_sums[:, SPAN:]

    def block(d):
        return g2.at[pl.ds(pl.multiple_of(d * FIN_ROWS, 8), FIN_ROWS)]

    each(NZ, lambda p: copy("rs", p, block((z + p) % NZ), rs.at[z], to_z(p)).start())
    rs[z] = g2[pl.ds(pl.multiple_of(z * FIN_ROWS, 8), FIN_ROWS), :]

    each(NG, lambda p: copy("xg", p, xp, xg.at[(g + NG - p) % NG], to_g(p)).wait_recv())
    each(NZ, lambda p: copy("gp", p, gp_src, gp_all.at[(z + NZ - p) % NZ], to_z(p)).wait_recv())
    dw = jnp.zeros((SPAN, SPAN), f32)
    for t in range(8):
        dw = dw + dot(xg[:, t].reshape(SPAN, SPAN), gp_all[2 * t:2 * t + 2].reshape(SPAN, SPAN))
    dw_src[...] = dw.reshape(NG, 16, SPAN)
    each(NG, lambda p: copy("dw", p, dw_src.at[(g + p) % NG], dw_in.at[g], to_g(p)).start())
    dw_in[g] = dw_src[g]

    each(NZ, lambda p: copy("rs", p, block((z + p) % NZ), rs.at[(z + NZ - p) % NZ], to_z(p)).wait_recv())
    y1[y] = jnp.sum(rs[...], axis=0)
    each(NY, lambda p: copy("y1", p, y1.at[y], y1.at[y], to_y(p)).start())

    each(NG, lambda p: copy("dw", p, dw_src.at[(g + p) % NG], dw_in.at[(g + NG - p) % NG], to_g(p)).wait_recv())
    y2[y] = dw_in[...]
    each(NY, lambda p: copy("y2", p, y2.at[y], y2.at[y], to_y(p)).start())

    each(NY, lambda p: copy("y1", p, y1.at[y], y1.at[(y + NY - p) % NY], to_y(p)).wait_recv())
    fin = jnp.sum(y1[...], axis=0)
    fin_16 = fin.astype(bf16)
    low_part = (fin[8:16] - fin_16[8:16].astype(f32)).astype(bf16)
    full[c, x, z] = jnp.concatenate([fin_16.astype(f32), low_part.astype(f32)], axis=0).astype(bf16)
    here = full.at[c, x, z]
    each(NZ, lambda p: copy("fz", p, here, here, to_z(p)).start())

    each(NY, lambda p: copy("y2", p, y2.at[y], y2.at[(y + NY - p) % NY], to_y(p)).wait_recv())
    g1 = jnp.sum(y2[...], axis=0)
    for d in range(NG):
        g1s_out[:, d * SPAN:(d + 1) * SPAN] = g1[d, 0:COLS]
        g1n_out[:, d * SPAN:(d + 1) * SPAN] = g1[d, COLS:2 * COLS]

    each(NZ, lambda p: copy("fz", p, here, full.at[c, x, (z + NZ - p) % NZ], to_z(p)).wait_recv())
    column_x = full.at[c, x]
    each(NX, lambda p: copy("fx", p, column_x, column_x, to_x(p)).start())
    each(NX, lambda p: copy("fx", p, column_x, full.at[c, (x + NX - p) % NX], to_x(p)).wait_recv())
    to_core = {"cols": z * NG + x * 2 + (1 - c), "rep": y}
    copy("fc", 0, full.at[c], full.at[c], to_core).start()
    copy("fc", 0, full.at[c], full.at[1 - c], to_core).wait_recv()

    for d in range(NG):
        got = full[d % 2, d // 2].astype(f32)
        flat = got[:, 0:FIN_ROWS].reshape(NZ * FIN_ROWS, SPAN)
        cut = slice(d * SPAN, (d + 1) * SPAN)
        g2s_out[:, cut] = flat[0:CLASSES]
        g2n_out[:, cut] = flat[160:160 + CLASSES]
        tail = flat[320:328] + got[13, 24:32]
        gb1_out[d:d + 1, :] = tail[0:1]
        if d == 0:
            gb2_out[:, 0:SPAN] = tail[1:2]
            gb2_out[:, SPAN:CLASSES] = tail[2:3, 0:CLASSES - SPAN]
            loss_out[...] = tail[2:3, LOSS_LANE - SPAN:LOSS_LANE - SPAN + 1] / targets

    each(NG, lambda p: copy("w_g", p, w_src.at[(g + p) % NG], w_mid.at[g], to_g(p)).wait_send())
    each(NG, lambda p: copy("aux", p, aux.at[g], aux.at[g], to_g(p)).wait_send())
    each(NZ, lambda p: copy("w_z", p, w_all.at[z], w_all.at[z], to_z(p)).wait_send())
    each(NZ, lambda p: copy("x_z", p, x_src.at[(z + p) % NZ], x_in.at[z], to_z(p)).wait_send())
    each(NG, lambda p: copy("x_g", p, x_mid, x_all.at[g], to_g(p)).wait_send())
    each(NG, lambda p: copy("xg", p, xp, xg.at[g], to_g(p)).wait_send())
    each(NG, lambda p: copy("lr", p, lp.at[(g + p) % NG], lr.at[g], to_g(p)).wait_send())
    each(NG, lambda p: copy("gl", p, gl_src, gl_all.at[g], to_g(p)).wait_send())
    each(NZ, lambda p: copy("gp", p, gp_src, gp_all.at[z], to_z(p)).wait_send())
    each(NZ, lambda p: copy("rs", p, block((z + p) % NZ), rs.at[z], to_z(p)).wait_send())
    each(NG, lambda p: copy("dw", p, dw_src.at[(g + p) % NG], dw_in.at[g], to_g(p)).wait_send())
    each(NY, lambda p: copy("y1", p, y1.at[y], y1.at[y], to_y(p)).wait_send())
    each(NY, lambda p: copy("y2", p, y2.at[y], y2.at[y], to_y(p)).wait_send())
    each(NZ, lambda p: copy("fz", p, here, here, to_z(p)).wait_send())
    each(NX, lambda p: copy("fx", p, column_x, column_x, to_x(p)).wait_send())
    copy("fc", 0, full.at[c], full.at[c], to_core).wait_send()


def per_device(
    features, self_ids, nbr_ids, nbr_counts, w1_self, w1_nbr, bias1, w2_self, w2_nbr, bias2, labels, top_ids, top_counts
):
    hidden = bias1.shape[0]
    shapes = (
        ((1, 1), f32), ((COLS, hidden), f32), ((COLS, hidden), f32), ((NG, SPAN), f32),
        ((CLASSES, hidden), f32), ((CLASSES, hidden), f32), ((1, CLASSES), f32),
    )
    scratch = [
        VMEM((LOW // SPAN, HIGH * 8, SPAN), f32),
        VMEM((HIGH * COLS, LOW), bf16),
        VMEM((16, hidden), f32),
        VMEM((NG, 16, SPAN), bf16),
        VMEM((NG, 16, SPAN), bf16),
        VMEM((NZ, SPAN, SPAN), bf16),
        VMEM((NG, 8, SPAN), f32),
        VMEM((8, SPAN, SPAN), f32),
        VMEM((8 * SPAN, SPAN), f32),
        VMEM((8, 16, SPAN), bf16),
        VMEM((NZ, 16, SPAN), bf16),
        VMEM((NZ, 16, SPAN), bf16),
        VMEM((8, 16, SPAN), bf16),
        VMEM((NG, 8, 16, SPAN), bf16),
        VMEM((NG, 8, 16, SPAN), bf16),
        VMEM((NG, 8, 2 * SPAN), f32),
        VMEM((NG, 8, 2 * SPAN), f32),
        VMEM((8, 2 * SPAN), f32),
        VMEM((NG, 8, 2 * SPAN), f32),
        VMEM((64, SPAN), bf16),
        VMEM((NZ, 64, SPAN), bf16),
        VMEM((NZ * FIN_ROWS, SPAN), f32),
        VMEM((NZ, FIN_ROWS, SPAN), f32),
        VMEM((NY, FIN_ROWS, SPAN), f32),
        VMEM((2, NX, NZ, 32, SPAN), bf16),
        VMEM((NG, 16, SPAN), f32),
        VMEM((NG, 16, SPAN), f32),
        VMEM((NY, NG, 16, SPAN), f32),
        pltpu.SemaphoreType.DMA((total_sems,)),
        pltpu.SemaphoreType.DMA((total_sems,)),
    ]
    loss, g1s, g1n, gb1, g2s, g2n, gb2 = pl.pallas_call(
        step_kernel,
        out_shape=[jax.ShapeDtypeStruct(s, t) for s, t in shapes],
        in_specs=[pl.BlockSpec(memory_space=VMEM)] * 13,
        out_specs=[pl.BlockSpec(memory_space=VMEM)] * 7,
        scratch_shapes=scratch,
        compiler_params=pltpu.CompilerParams(
            collective_id=0, has_side_effects=True, vmem_limit_bytes=48 * 2**20
        ),
        name="step",
    )(
        features.T, self_ids.T, jnp.transpose(nbr_ids, (2, 1, 0)), nbr_counts.T, w1_self, w1_nbr,
        bias1.reshape(NG, SPAN), w2_self.T, w2_nbr.T, bias2.reshape(1, CLASSES), labels.reshape(1, 8),
        top_ids, top_counts.reshape(1, 8),
    )
    return loss.reshape(()), g1s, g1n, gb1.reshape(hidden), g2s.T, g2n.T, gb2.reshape(CLASSES)


def solution(mesh):
    in_specs = (
        P(None, "cols"), P(None, "rep"), P(None, "rep", None), P(None, "rep"), P("cols", None), P("cols", None),
        P(), P(), P(), P(), P(("cols", "rep")), P(("cols", "rep"), None), P(("cols", "rep")),
    )
    out_specs = (P(), P("cols", None), P("cols", None), P(), P(), P(), P())
    return jax.shard_map(per_device, mesh=mesh, in_specs=in_specs, out_specs=out_specs, check_vma=False)
```

time: 1030 us -> 135 us (0.13)
  waiting for transfers between devices: 743 us -> 0 us
  blocking collectives: 127 us -> 0 us
  Pallas kernels: 0 us -> 120 us
  local copies, waits for them, and re-layouts: 132 us -> 12.3 us
  between operations: 15.7 us -> 2.38 us
  matrix products: 12.4 us -> 0 us
    psum x1 -> x0, waiting for transfers between devices: 452 us -> none  [per_device(): lax.psum((jnp.sum(row_loss), local_w2_self, local_w2_nbr, local_bias2, lo...]
    reduce_scatter x1 -> x0, waiting for transfers between devices: 258 us -> none  [per_device(): lax.psum_scatter(jnp.dot(rows_self, w1_self, preferred_element_type=jnp.f...]
    psum x2 -> x0, blocking collectives: 127 us -> none  [the longest x1 113 us: per_device(): lax.psum((jnp.sum(row_loss), local_w2_self, local_w2_nbr, local_bias2, lo...]
    pallas_call x0 -> x1, Pallas kernels: none -> 120 us  [per_device(): pl.pallas_call(step_kernel, out_shape=[jax.ShapeDtypeStruct(s, t) for s,...]
    gather x4 -> x0, local copies, waits for them, and re-layouts: 113 us -> none  [the longest x3 102 us: per_device(): jnp.take(features, nbr_ids.reshape(group_rows * fanout), axis=0)]
    all_gather x1 -> x0, waiting for transfers between devices: 32.5 us -> none  [per_device(): pieces = lax.all_gather(grad_pre, 'cols', axis=0, tiled=True)]
    dot_general x12 -> x0, matrix products: 12.4 us -> none  [the longest x4 6.41 us: contract_rows(): lax.dot_general(left, right, (((0,), (0,)), ((), ())), preferred_element_...]
  transfers between devices with their start and end apart: 3 -> 0, of which waited for: 3 -> 0; matrix products, arithmetic and copies ran while one was open for 1% -> 0% of each run, Pallas kernels for 0% -> 0%
where the time goes in v1:
time: 135 us; the launch traced here: 134 us
  Pallas kernels  120 us (89%)
  local copies, waits for them, and re-layouts  12.3 us (9%)
  between operations  2.38 us (2%)
    pallas_call x1, Pallas kernels, per_device(): pl.pallas_call(step_kernel, out_shape=[jax.ShapeDtypeStruct(s, t) for s,...  120 us
    unnamed x32, local copies, waits for them, and re-layouts  12.3 us

profile of v1, /device:TPU:1, one launch (start us, length us, event | category | flops | bytes accessed | tf_op | source)
XLA Modules:
  0.0 134.5 jit_solution(13048642323566954731)
XLA Ops:
  0.6 0.0 copy-start.4
  0.6 0.0 copy-start.12
  0.7 0.0 copy-start.10
  0.7 0.0 copy-start.11
  0.7 0.7 copy-done.4
  1.4 0.0 copy-done.12
  1.4 0.0 copy-done.10
  1.4 0.0 copy-done.11
  1.4 0.0 copy-start
  1.4 1.2 copy-done
  2.6 0.0 copy-start.1
  2.6 1.0 copy-done.1
  3.6 0.0 copy-start.2
  3.6 1.0 copy-done.2
  4.5 0.0 copy-start.3
  4.5 0.9 copy-done.3
  5.4 0.0 copy-start.5
  5.4 0.7 copy-done.5
  6.1 0.0 copy-start.6
  6.2 0.7 copy-done.6
  6.8 0.0 copy-start.7
  6.8 0.7 copy-done.7
  7.5 0.0 copy-start.8
  7.5 0.7 copy-done.8
  8.2 0.0 copy-start.9
  8.2 0.7 copy-done.9
  8.9 119.8 %step.1 = (f32[1,1]{1,0:T(1,128)}, f32[6,1024]{1,0:T(8,128)S(1)}, f32[6,1024]{1,0:T(8,128)S(1)}, f32[8,128]{1,0:T(8,128)S(1)}, f32[153,1024]{1,0:T(8,128)S(1)}, ...) custom-call(bf16[6,65536]{1,0:T(8,128)(2,1)S(1)} %bitcast.15, s32[8,128]{1,0:T(8,128)S(1)} %bitcast.21, ...), custom_call_target="tpu_custom_call" | custom-call | tf_op jit(solution)/shard_map/step/pallas_call | solution.py:353
  129.3 0.6 copy.28
  129.9 0.6 copy.29
  130.5 0.6 copy.30
  131.1 0.8 copy.31
  131.9 0.8 copy.32
  132.8 0.6 copy.33
Async XLA Ops:
  0.6 0.7 copy-start.4
  0.6 0.7 copy-start.12
  0.7 0.7 copy-start.10
  0.7 0.7 copy-start.11
  1.4 1.2 copy-start
  2.6 1.0 copy-start.1
  3.6 1.0 copy-start.2
  4.5 0.9 copy-start.3
  5.4 0.7 copy-start.5
  6.1 0.7 copy-start.6
  6.8 0.7 copy-start.7
  7.5 0.7 copy-start.8
  8.2 0.7 copy-start.9

commit v2 on v0

v2 whole, which is shorter than its diff:
```python
import jax
import jax.numpy as jnp
from jax import lax
from jax.experimental import pallas as pl
from jax.experimental.pallas import tpu as pltpu
from jax.sharding import PartitionSpec as P

f32, bf16 = jnp.float32, jnp.bfloat16
loss_scale = 64.0

NZ, NG, NY, NX = 16, 8, 4, 4
TARGETS = 8 * NZ * NG * NY
LOW = 512
HIGH = 65536 // LOW
COLS = 6
FAN = 25
CLASSES = 153
LOSS_LANE = 200
SPAN = 128
NP = NX * NY
NBR_AT = 159
TAIL_AT = 312
GRAD_ROWS = 320
PART = GRAD_ROWS // NY
TILES = PART // 8
VMEM = pltpu.VMEM

SEMS = {}
total_sems = 0
for stage, slots in (
    ("w_g", NG), ("aux", NG), ("w_z", NZ), ("x_z", NZ), ("x_g", NG), ("xg", NG), ("lr", NG), ("gl", NG),
    ("gp_far", 4), ("gp_near", 4), ("ry", NY), ("rz", NZ), ("az", NZ), ("plane", NP), ("core", NP),
    ("dw", NG), ("y2", NY),
):
    SEMS[stage] = total_sems
    total_sems += slots


def dot(a, b, ca=1, cb=0):
    return lax.dot_general(a, b, (((ca,), (cb,)), ((), ())), preferred_element_type=f32)


def iota(shape, dim):
    return lax.broadcasted_iota(jnp.int32, shape, dim)


def step_kernel(
    feat_hbm, self_hbm, nbr_hbm, counts_hbm, w1s_hbm, w1n_hbm, bias1_hbm, w2s_hbm, w2n_hbm, bias2_hbm, labels_hbm,
    top_hbm, top_counts_hbm, full, g1_out,
    feat, self_ids, nbr_ids, nbr_counts, w1s, w1n, bias1, w2s, w2n, bias2, labels, top_ids, top_counts,
    split, table, wt, w_src, w_mid, w_all, aux, rows_t, rows_m, xp, x_src, x_in, x_mid, x_all, xg,
    lp, lr, gl_src, gl_all, gp_all, g2, ra, r1, rb, rc, dw_src, dw_in, y2, send_sem, recv_sem, load_sem,
):
    o = lax.axis_index("cols")
    y = lax.axis_index("rep")
    z = o // NG
    g = o % NG
    x = g // 2
    c = g % 2
    here = x * NY + y

    def to_z(p):
        return {"cols": ((z + p) % NZ) * NG + g, "rep": y}

    def to_g(p):
        return {"cols": z * NG + (g + p) % NG, "rep": y}

    def to_y(p):
        return {"cols": o, "rep": (y + p) % NY}

    def to_plane(p):
        q = (here + p) % NP
        return {"cols": z * NG + (q // NY) * 2 + c, "rep": q % NY}

    to_core = {"cols": z * NG + x * 2 + (1 - c), "rep": y}

    def copy(stage, p, src, dst, device):
        at = SEMS[stage] + p
        return pltpu.make_async_remote_copy(
            src_ref=src, dst_ref=dst, send_sem=send_sem.at[at], recv_sem=recv_sem.at[at], device_id=device
        )

    def each(n, body, first=1):
        def run(p, carry):
            body(p)
            return carry
        lax.fori_loop(first, n, run, 0)

    loads = [
        pltpu.make_async_copy(src, dst, load_sem.at[i])
        for i, (src, dst) in enumerate((
            (w1s_hbm, w1s), (w1n_hbm, w1n), (top_counts_hbm, top_counts), (labels_hbm, labels), (top_hbm, top_ids),
            (feat_hbm, feat), (self_hbm, self_ids), (counts_hbm, nbr_counts), (nbr_hbm, nbr_ids),
            (bias1_hbm, bias1), (bias2_hbm, bias2), (w2s_hbm, w2s), (w2n_hbm, w2n),
        ))
    ]
    for load in loads:
        load.start()

    barrier = pltpu.get_barrier_semaphore()
    each(NZ, lambda p: pl.semaphore_signal(barrier, inc=1, device_id=to_z(p)))
    each(NG, lambda p: pl.semaphore_signal(barrier, inc=1, device_id=to_g(p)))

    def signal_plane(p):
        device = {"cols": z * NG + (p // (NY - 1)) * 2 + c, "rep": (y + 1 + p % (NY - 1)) % NY}
        pl.semaphore_signal(barrier, inc=1, device_id=device)

    each(NX * (NY - 1), signal_plane, 0)

    with jax.named_scope("prepare"):
        wt[...] = jnp.zeros_like(wt)
        for load in loads[0:5]:
            load.wait()
        wt[0:COLS, :] = w1s[...].astype(f32)
        wt[COLS:2 * COLS, :] = w1n[...].astype(f32)
        for d in range(NG):
            w_src[d] = wt[:, d * SPAN:(d + 1) * SPAN].astype(bf16)
        w_mid[g] = w_src[g]

        eye = iota((8, 8), 0) == iota((8, 8), 1)

        def column(ref):
            return jnp.sum(jnp.where(eye, jnp.broadcast_to(ref[...].astype(f32), (8, 8)), 0.0), axis=1, keepdims=True)

        count_col = column(top_counts)
        label_col = column(labels)
        picks = top_ids[...]
        live_top = iota(picks.shape, 1).astype(f32) < count_col
        lane = iota((8, SPAN), 1)
        mine = jnp.where(lane == 8, count_col, jnp.where(lane == 9, label_col, 0.0))
        for s in range(8):
            n_s = jnp.sum(jnp.where(live_top & (picks == s), 1.0, 0.0), axis=1, keepdims=True)
            mine = jnp.where(lane == s, n_s, mine)
        aux[g] = mine

    with jax.named_scope("barrier"):
        pl.semaphore_wait(barrier, NZ - 1 + NG - 1 + NX * (NY - 1))

    each(NG, lambda p: copy("w_g", p, w_src.at[(g + p) % NG], w_mid.at[g], to_g(p)).start())
    each(NG, lambda p: copy("aux", p, aux.at[g], aux.at[g], to_g(p)).start())

    with jax.named_scope("table"):
        loads[5].wait()

        def split_high(h, carry):
            piece = feat[:, pl.ds(pl.multiple_of(h * LOW, LOW), LOW)].astype(f32)
            for q in range(LOW // SPAN):
                split[q, pl.ds(pl.multiple_of(h * 8, 8), COLS), :] = piece[:, q * SPAN:(q + 1) * SPAN]
            return carry

        lax.fori_loop(0, HIGH, split_high, 0, unroll=8)
        for k in range(COLS):
            for q in range(LOW // SPAN):
                table[k * HIGH:(k + 1) * HIGH, q * SPAN:(q + 1) * SPAN] = (
                    split[q, pl.ds(k, HIGH, stride=8), :].astype(bf16)
                )

    with jax.named_scope("weights"):
        each(NG, lambda p: copy("w_g", p, w_src.at[(g + p) % NG], w_mid.at[(g + NG - p) % NG], to_g(p)).wait_recv())
        w_all[z] = w_mid[...].reshape(SPAN, SPAN)
        each(NZ, lambda p: copy("w_z", p, w_all.at[z], w_all.at[z], to_z(p)).start())

    with jax.named_scope("lookup"):
        for load in loads[6:9]:
            load.wait()
        io_low = iota((LOW, SPAN), 0)
        io_high = iota((HIGH, SPAN), 0)
        counts = nbr_counts[...]

        def look(ids, alive):
            low = jnp.bitwise_and(ids, LOW - 1)
            high = jnp.where(alive, jnp.right_shift(ids, LOW.bit_length() - 1), -1)
            hot = jnp.concatenate([(io_low == low[j:j + 1, :]).astype(f32).astype(bf16) for j in range(8)], axis=1)
            mask = jnp.concatenate([io_high == high[j:j + 1, :] for j in range(8)], axis=1)
            got = dot(table[...], hot)
            return tuple(
                jnp.sum(jnp.where(mask, got[k * HIGH:(k + 1) * HIGH], 0.0).reshape(HIGH // 8, 8, 8 * SPAN), axis=0)
                for k in range(COLS)
            )

        own = look(self_ids[...], counts > 0)

        def add_nbr(k, sums):
            return tuple(a + b for a, b in zip(sums, look(nbr_ids[k], counts > k)))

        sums = lax.fori_loop(0, FAN, add_nbr, tuple(jnp.zeros((8, 8 * SPAN), f32) for _ in range(COLS)), unroll=5)

    with jax.named_scope("rows"):
        rows_t[...] = jnp.zeros_like(rows_t)
        for j in range(8):
            cut = slice(j * SPAN, (j + 1) * SPAN)
            count = counts[j:j + 1, :].astype(f32)
            for k in range(COLS):
                rows_t[j, k:k + 1, :] = jnp.sum(own[k][:, cut], axis=0, keepdims=True)
                rows_t[j, COLS + k:COLS + k + 1, :] = jnp.sum(sums[k][:, cut], axis=0, keepdims=True) / count
            rows_t[j, 2 * COLS:2 * COLS + 1, :] = jnp.ones((1, SPAN), f32)
        for j in range(8):
            rows_m[pl.ds(j, SPAN, stride=8), :] = rows_t[j].T
        for t in range(8):
            xp[t] = rows_m[t * SPAN:(t + 1) * SPAN, :].T[0:16, :].astype(bf16)

        odd = z % 2
        half = iota((16, SPAN), 1) // 64
        for t in range(8):
            straight = xp[t].astype(f32)
            turned = pltpu.roll(straight, 64, 1)
            x_src[2 * t] = jnp.where(half == odd, jnp.where(odd == 0, straight, turned), 0.0).astype(bf16)
            x_src[2 * t + 1] = jnp.where(half == odd, jnp.where(odd == 1, straight, turned), 0.0).astype(bf16)
        each(NZ, lambda p: copy("x_z", p, x_src.at[(z + p) % NZ], x_in.at[z], to_z(p)).start())
        x_in[z] = x_src[z]
        xg[g] = xp[...]

    with jax.named_scope("lists"):
        each(NG, lambda p: copy("aux", p, aux.at[g], aux.at[(g + NG - p) % NG], to_g(p)).wait_recv())
        lists = aux[...].reshape(64, SPAN)
        top_div = lists[:, 8:9]
        spread = (iota((SPAN, 64), 0) == iota((SPAN, 64), 1) % 8).astype(f32).astype(bf16)
        same = iota((64, 64), 0) // 8 == iota((64, 64), 1) // 8
        picked = jnp.where(same, dot(lists.astype(bf16), spread), 0.0).astype(bf16)
        for load in loads[9:]:
            load.wait()

    with jax.named_scope("rows_to_z"):
        each(NZ, lambda p: copy("x_z", p, x_src.at[(z + p) % NZ], x_in.at[(z + NZ - p) % NZ], to_z(p)).wait_recv())
    for t in range(8):
        x_mid[t] = x_in[2 * t] + x_in[2 * t + 1]
    each(NG, lambda p: copy("x_g", p, x_mid, x_all.at[g], to_g(p)).start())
    each(NG, lambda p: copy("xg", p, xp, xg.at[g], to_g(p)).start())
    x_all[g] = x_mid[...]

    with jax.named_scope("weights_over_z"):
        each(NZ, lambda p: copy("w_z", p, w_all.at[z], w_all.at[(z + NZ - p) % NZ], to_z(p)).wait_recv())
    with jax.named_scope("rows_over_g"):
        each(NG, lambda p: copy("x_g", p, x_mid, x_all.at[(g + NG - p) % NG], to_g(p)).wait_recv())

    with jax.named_scope("layers"):
        both = jnp.zeros((SPAN, 2 * SPAN), f32)
        for t in range(8):
            left = x_all[:, t].reshape(SPAN, SPAN)
            right = jnp.concatenate([w_all[2 * t], w_all[2 * t + 1]], axis=1)
            both = both + dot(left, right, 0, 0)
        pre = both[0:64, 0:SPAN] + both[64:SPAN, SPAN:] + bias1[pl.ds(g, 1), :]
        hidden = jnp.maximum(pre, 0.0).astype(bf16)
        top_mean = (dot(picked, hidden) / top_div).astype(bf16)
        span = pl.ds(pl.multiple_of(g * SPAN, SPAN), SPAN)
        w2s_g = w2s[:, span]
        w2n_g = w2n[:, span]
        part = dot(hidden, w2s_g, 1, 1) + dot(top_mean, w2n_g, 1, 1)
        lp[...] = jnp.zeros_like(lp)
        lp[:, :, 0:CLASSES] = part.reshape(NG, 8, CLASSES)
        each(NG, lambda p: copy("lr", p, lp.at[(g + p) % NG], lr.at[g], to_g(p)).start())
        lr[g] = lp[g]
    with jax.named_scope("logits_wait"):
        each(NG, lambda p: copy("lr", p, lp.at[(g + p) % NG], lr.at[(g + NG - p) % NG], to_g(p)).wait_recv())

    with jax.named_scope("softmax"):
        logits = jnp.sum(lr[...], axis=0)[:, 0:CLASSES] + bias2[...]
        exps = jnp.exp(logits)
        total = jnp.sum(exps, axis=1, keepdims=True)
        onehot = jnp.where(iota((8, CLASSES), 1).astype(f32) == label_col, 1.0, 0.0)
        row_loss = jnp.log(total) - jnp.sum(onehot * logits, axis=1, keepdims=True)
        grad = ((exps / total - onehot) * (loss_scale / TARGETS)).astype(bf16)
        gl_src[...] = jnp.where(iota((8, 2 * SPAN), 1) == LOSS_LANE, row_loss, 0.0)
        gl_src[:, 0:CLASSES] = grad.astype(f32)
        each(NG, lambda p: copy("gl", p, gl_src, gl_all.at[g], to_g(p)).start())
        gl_all[g] = gl_src[...]
        g2[...] = jnp.zeros_like(g2)
    with jax.named_scope("grad_logits_wait"):
        each(NG, lambda p: copy("gl", p, gl_src, gl_all.at[(g + NG - p) % NG], to_g(p)).wait_recv())

    with jax.named_scope("classifier_grads"):
        gl_rows = gl_all[...].reshape(64, 2 * SPAN)
        gl = gl_rows[:, 0:CLASSES].astype(bf16)
        g2[0:CLASSES, :] = dot(gl, hidden, 0, 0)
        g2[NBR_AT:NBR_AT + CLASSES, :] = dot(gl, top_mean, 0, 0)
        col_sums = jnp.sum(gl_rows, axis=0, keepdims=True)
        g2[TAIL_AT:TAIL_AT + 1, :] = col_sums[:, 0:SPAN]
        g2[TAIL_AT + 1:TAIL_AT + 2, :] = col_sums[:, SPAN:]

        def block(d):
            return g2.at[pl.ds(pl.multiple_of(d * PART, 8), PART)]

        each(NY, lambda p: copy("ry", p, block((y + p) % NY), ra.at[y], to_y(p)).start())
        ra[y] = g2[pl.ds(pl.multiple_of(y * PART, 8), PART), :]

    with jax.named_scope("back"):
        back_top = dot(gl, w2n_g) / top_div
        top_1 = back_top.astype(bf16)
        rest = back_top - top_1.astype(f32)
        top_2 = rest.astype(bf16)
        top_3 = (rest - top_2.astype(f32)).astype(bf16)
        back = dot(gl, w2s_g) + (dot(picked, top_1, 0, 0) + (dot(picked, top_2, 0, 0) + dot(picked, top_3, 0, 0)))
        grad_pre = jnp.where(pre > 0.0, back, 0.0).astype(bf16)
        row, col = z % 4, z // 4
        gp_all[row, col] = grad_pre
        mine_gp = gp_all.at[row, col]
        each(4, lambda p: copy("gp_far", p, mine_gp, mine_gp, to_z(4 * p)).start())

    with jax.named_scope("sum_over_rep"):
        each(NY, lambda p: copy("ry", p, block((y + p) % NY), ra.at[(y + NY - p) % NY], to_y(p)).wait_recv())
        r1[...] = jnp.sum(ra[...], axis=0)

        def tile(d):
            return r1.at[pl.ds(pl.multiple_of(d * 8, 8), 8)]

        def send_tile(p):
            d = (z + p) % NZ

            @pl.when(d < TILES)
            def _():
                copy("rz", p, tile(d), rb.at[z], to_z(p)).start()

        each(NZ, send_tile)

    with jax.named_scope("grad_pre_far"):
        each(4, lambda p: copy("gp_far", p, mine_gp, gp_all.at[row, (col + 4 - p) % 4], to_z(4 * p)).wait_recv())
    four = gp_all.at[row]
    near = (1, NZ - 1, 2)
    for i, p in enumerate(near):
        copy("gp_near", i, four, four, to_z(p)).start()

    with jax.named_scope("scatter_over_z"):
        @pl.when(z < TILES)
        def _():
            rb[z] = r1[pl.ds(pl.multiple_of(z * 8, 8), 8), :]
            each(NZ, lambda p: copy("rz", p, tile(z), rb.at[(z + NZ - p) % NZ], to_z(p)).wait_recv())
            rc[z] = jnp.sum(rb[...], axis=0)
            each(NZ, lambda p: copy("az", p, rc.at[z], rc.at[z], to_z(p)).start())

    with jax.named_scope("grad_pre_near"):
        each(NG, lambda p: copy("xg", p, xp, xg.at[(g + NG - p) % NG], to_g(p)).wait_recv())
        for i, p in enumerate(near):
            copy("gp_near", i, four, gp_all.at[(row + 4 - p % 4) % 4], to_z(p)).wait_recv()
    with jax.named_scope("layer_grads"):
        dw = jnp.zeros((SPAN, SPAN), f32)
        for t in range(8):
            pair = [gp_all[(2 * t + i) % 4, (2 * t + i) // 4] for i in range(2)]
            dw = dw + dot(xg[:, t].reshape(SPAN, SPAN), jnp.concatenate(pair, axis=0))
        dw_src[...] = dw.reshape(NG, 16, SPAN)
        each(NG, lambda p: copy("dw", p, dw_src.at[(g + p) % NG], dw_in.at[g], to_g(p)).start())
        dw_in[g] = dw_src[g]

    with jax.named_scope("gather_over_z"):
        def wait_tile(s, carry):
            @pl.when(s != z)
            def _():
                copy("az", (z + NZ - s) % NZ, rc.at[s], rc.at[s], to_z(1)).wait_recv()
            return carry

        lax.fori_loop(0, TILES, wait_tile, 0)
        fin = rc[...].reshape(PART, SPAN)
        low_part = fin - fin.astype(bf16).astype(f32)
        low_part = jnp.concatenate([low_part[0:2], low_part[0:PART - 2]], axis=0)
        at = iota((PART, SPAN), 0) - (TAIL_AT - (NY - 1) * PART)
        is_low = (y == NY - 1) & (at >= 2) & (at < 4)
        full[c, x, y] = jnp.where(is_low, low_part, fin).astype(bf16)
        out_block = full.at[c, x, y]
        each(NP, lambda p: copy("plane", p, out_block, out_block, to_plane(p)).start())
        copy("core", here, out_block, out_block, to_core).start()

    with jax.named_scope("layer_grads_wait"):
        each(NG, lambda p: copy("dw", p, dw_src.at[(g + p) % NG], dw_in.at[(g + NG - p) % NG], to_g(p)).wait_recv())
        y2[y] = dw_in[...]
        each(NY, lambda p: copy("y2", p, y2.at[y], y2.at[y], to_y(p)).start())

    with jax.named_scope("gather_over_plane"):
        def forward(p):
            q = (here + NP - p) % NP
            there = full.at[c, q // NY, q % NY]
            copy("plane", p, out_block, there, to_plane(p)).wait_recv()
            copy("core", q, there, there, to_core).start()

        each(NP, forward)

    with jax.named_scope("layer_grads_over_rep"):
        each(NY, lambda p: copy("y2", p, y2.at[y], y2.at[(y + NY - p) % NY], to_y(p)).wait_recv())
        g1_out[...] = jnp.sum(y2[...], axis=0)

    with jax.named_scope("gather_over_core"):
        def from_core(q):
            there = full.at[1 - c, q // NY, q % NY]
            copy("core", q, there, there, to_core).wait_recv()

        each(NP, from_core, 0)

    with jax.named_scope("sends"):
        each(NG, lambda p: copy("w_g", p, w_src.at[(g + p) % NG], w_mid.at[g], to_g(p)).wait_send())
        each(NG, lambda p: copy("aux", p, aux.at[g], aux.at[g], to_g(p)).wait_send())
        each(NZ, lambda p: copy("w_z", p, w_all.at[z], w_all.at[z], to_z(p)).wait_send())
        each(NZ, lambda p: copy("x_z", p, x_src.at[(z + p) % NZ], x_in.at[z], to_z(p)).wait_send())
        each(NG, lambda p: copy("x_g", p, x_mid, x_all.at[g], to_g(p)).wait_send())
        each(NG, lambda p: copy("xg", p, xp, xg.at[g], to_g(p)).wait_send())
        each(NG, lambda p: copy("lr", p, lp.at[(g + p) % NG], lr.at[g], to_g(p)).wait_send())
        each(NG, lambda p: copy("gl", p, gl_src, gl_all.at[g], to_g(p)).wait_send())
        each(4, lambda p: copy("gp_far", p, mine_gp, mine_gp, to_z(4 * p)).wait_send())
        for i, p in enumerate(near):
            copy("gp_near", i, four, four, to_z(p)).wait_send()
        each(NY, lambda p: copy("ry", p, block((y + p) % NY), ra.at[y], to_y(p)).wait_send())

        def sent_tile(p):
            d = (z + p) % NZ

            @pl.when(d < TILES)
            def _():
                copy("rz", p, tile(d), rb.at[z], to_z(p)).wait_send()

        each(NZ, sent_tile)

        @pl.when(z < TILES)
        def _():
            each(NZ, lambda p: copy("az", p, rc.at[z], rc.at[z], to_z(p)).wait_send())

        each(NP, lambda p: copy("plane", p, out_block, out_block, to_plane(p)).wait_send())
        each(NP, lambda q: copy("core", q, out_block, out_block, to_core).wait_send(), 0)
        each(NG, lambda p: copy("dw", p, dw_src.at[(g + p) % NG], dw_in.at[g], to_g(p)).wait_send())
        each(NY, lambda p: copy("y2", p, y2.at[y], y2.at[y], to_y(p)).wait_send())


def finish_kernel(full, g1, *refs):
    outs, bufs, sem = refs[0:7], refs[7:14], refs[14]
    loss, g1s, g1n, gb1, g2s, g2n, gb2 = bufs
    for d in range(NG):
        cut = slice(d * SPAN, (d + 1) * SPAN)
        flat = full[d % 2, d // 2].astype(f32).reshape(GRAD_ROWS, SPAN)
        g2s[:, cut] = flat[0:CLASSES]
        g2n[:, cut] = flat[NBR_AT:NBR_AT + CLASSES]
        g1s[:, cut] = g1[d, 0:COLS]
        g1n[:, cut] = g1[d, COLS:2 * COLS]
        gb1[d:d + 1, :] = g1[d, 2 * COLS:2 * COLS + 1]
        if d == 0:
            tail = flat[TAIL_AT:TAIL_AT + 2] + flat[TAIL_AT + 2:TAIL_AT + 4]
            gb2[:, 0:SPAN] = tail[0:1]
            gb2[:, SPAN:CLASSES] = tail[1:2, 0:CLASSES - SPAN]
            loss[...] = tail[1:2, LOSS_LANE - SPAN:LOSS_LANE - SPAN + 1] / TARGETS
    stores = [pltpu.make_async_copy(b, r, sem.at[i]) for i, (b, r) in enumerate(zip(bufs, outs))]
    for store in stores:
        store.start()
    for store in stores:
        store.wait()


def per_device(
    features, self_ids, nbr_ids, nbr_counts, w1_self, w1_nbr, bias1, w2_self, w2_nbr, bias2, labels, top_ids, top_counts
):
    hidden = bias1.shape[0]
    operands = (
        features.T, self_ids.T, jnp.transpose(nbr_ids, (2, 1, 0)), nbr_counts.T, w1_self, w1_nbr,
        bias1.reshape(NG, SPAN), w2_self.T, w2_nbr.T, bias2.reshape(1, CLASSES), labels.reshape(1, 8),
        top_ids, top_counts.reshape(1, 8),
    )
    scratch = [VMEM(a.shape, a.dtype) for a in operands] + [
        VMEM((LOW // SPAN, HIGH * 8, SPAN), f32),
        VMEM((HIGH * COLS, LOW), bf16),
        VMEM((16, hidden), f32),
        VMEM((NG, 16, SPAN), bf16),
        VMEM((NG, 16, SPAN), bf16),
        VMEM((NZ, SPAN, SPAN), bf16),
        VMEM((NG, 8, SPAN), f32),
        VMEM((8, SPAN, SPAN), f32),
        VMEM((8 * SPAN, SPAN), f32),
        VMEM((8, 16, SPAN), bf16),
        VMEM((NZ, 16, SPAN), bf16),
        VMEM((NZ, 16, SPAN), bf16),
        VMEM((8, 16, SPAN), bf16),
        VMEM((NG, 8, 16, SPAN), bf16),
        VMEM((NG, 8, 16, SPAN), bf16),
        VMEM((NG, 8, 2 * SPAN), f32),
        VMEM((NG, 8, 2 * SPAN), f32),
        VMEM((8, 2 * SPAN), f32),
        VMEM((NG, 8, 2 * SPAN), f32),
        VMEM((4, 4, 64, SPAN), bf16),
        VMEM((GRAD_ROWS, SPAN), f32),
        VMEM((NY, PART, SPAN), f32),
        VMEM((PART, SPAN), f32),
        VMEM((NZ, 8, SPAN), f32),
        VMEM((TILES, 8, SPAN), f32),
        VMEM((NG, 16, SPAN), f32),
        VMEM((NG, 16, SPAN), f32),
        VMEM((NY, NG, 16, SPAN), f32),
        pltpu.SemaphoreType.DMA((total_sems,)),
        pltpu.SemaphoreType.DMA((total_sems,)),
        pltpu.SemaphoreType.DMA((len(operands),)),
    ]
    full, g1 = pl.pallas_call(
        step_kernel,
        out_shape=[
            jax.ShapeDtypeStruct((2, NX, NY, PART, SPAN), bf16), jax.ShapeDtypeStruct((NG, 16, SPAN), f32),
        ],
        in_specs=[pl.BlockSpec(memory_space=pltpu.HBM)] * len(operands),
        out_specs=[pl.BlockSpec(memory_space=VMEM)] * 2,
        scratch_shapes=scratch,
        compiler_params=pltpu.CompilerParams(
            collective_id=0, has_side_effects=True, vmem_limit_bytes=60 * 2**20
        ),
        name="step",
    )(*operands)
    shapes = (
        (1, 1), (COLS, hidden), (COLS, hidden), (NG, SPAN), (CLASSES, hidden), (CLASSES, hidden), (1, CLASSES),
    )
    loss, g1s, g1n, gb1, g2s, g2n, gb2 = pl.pallas_call(
        finish_kernel,
        out_shape=[jax.ShapeDtypeStruct(s, f32) for s in shapes],
        in_specs=[pl.BlockSpec(memory_space=VMEM)] * 2,
        out_specs=[pl.BlockSpec(memory_space=pltpu.HBM)] * len(shapes),
        scratch_shapes=[VMEM(s, f32) for s in shapes] + [pltpu.SemaphoreType.DMA((len(shapes),))],
        name="finish",
    )(full, g1)
    return loss.reshape(()), g1s, g1n, gb1.reshape(hidden), g2s.T, g2n.T, gb2.reshape(CLASSES)


def solution(mesh):
    in_specs = (
        P(None, "cols"), P(None, "rep"), P(None, "rep", None), P(None, "rep"), P("cols", None), P("cols", None),
        P(), P(), P(), P(), P(("cols", "rep")), P(("cols", "rep"), None), P(("cols", "rep")),
    )
    out_specs = (P(), P("cols", None), P("cols", None), P(), P(), P(), P())
    return jax.shard_map(per_device, mesh=mesh, in_specs=in_specs, out_specs=out_specs, check_vma=False)
```

time: 1030 us -> 103 us (0.10)
  waiting for transfers between devices: 743 us -> 0 us
  local copies, waits for them, and re-layouts: 132 us -> 0 us
  blocking collectives: 127 us -> 0 us
  Pallas kernels: 0 us -> 102 us
  between operations: 15.7 us -> 0.65 us
  matrix products: 12.4 us -> 0 us
    psum x1 -> x0, waiting for transfers between devices: 452 us -> none  [per_device(): lax.psum((jnp.sum(row_loss), local_w2_self, local_w2_nbr, local_bias2, lo...]
    reduce_scatter x1 -> x0, waiting for transfers between devices: 258 us -> none  [per_device(): lax.psum_scatter(jnp.dot(rows_self, w1_self, preferred_element_type=jnp.f...]
    psum x2 -> x0, blocking collectives: 127 us -> none  [the longest x1 113 us: per_device(): lax.psum((jnp.sum(row_loss), local_w2_self, local_w2_nbr, local_bias2, lo...]
    gather x4 -> x0, local copies, waits for them, and re-layouts: 113 us -> none  [the longest x3 102 us: per_device(): jnp.take(features, nbr_ids.reshape(group_rows * fanout), axis=0)]
    pallas_call x0 -> x2, Pallas kernels: none -> 102 us  [the longest x1 99.6 us: per_device(): pl.pallas_call(step_kernel, out_shape=[jax.ShapeDtypeStruct((2, NX, NY, P...]
    all_gather x1 -> x0, waiting for transfers between devices: 32.5 us -> none  [per_device(): pieces = lax.all_gather(grad_pre, 'cols', axis=0, tiled=True)]
    unnamed x26 -> x0, local copies, waits for them, and re-layouts: 18.5 us -> none
    dot_general x12 -> x0, matrix products: 12.4 us -> none  [the longest x4 6.41 us: contract_rows(): lax.dot_general(left, right, (((0,), (0,)), ((), ())), preferred_element_...]
  transfers between devices with their start and end apart: 3 -> 0, of which waited for: 3 -> 0; matrix products, arithmetic and copies ran while one was open for 1% -> 0% of each run, Pallas kernels for 0% -> 0%
where the time goes in v2:
time: 103 us
  Pallas kernels  102 us (99%)
    pallas_call x1, Pallas kernels, per_device(): pl.pallas_call(step_kernel, out_shape=[jax.ShapeDtypeStruct((2, NX, NY, P...  99.6 us
    pallas_call x1, Pallas kernels, per_device(): pl.pallas_call(finish_kernel, out_shape=[jax.ShapeDtypeStruct(s, f32) for...  2.39 us

profile of v2, /device:TPU:1, one launch (start us, length us, event | category | flops | bytes accessed | tf_op | source)
XLA Modules:
  0.0 102.6 jit_solution(3546095896923007442)
XLA Ops:
  0.6 99.6 %step.1 = (bf16[2,4,4,80,128]{4,3,2,1,0:T(8,128)(2,1)}, f32[8,16,128]{2,1,0:T(8,128)}) custom-call(bf16[6,65536]{1,0:T(8,128)(2,1)} %bitcast.15, s32[8,128]{1,0:T(8,128)} %bitcast.19, s32[25,8,128]{2,1,0:T(8,128)} %bitcast.18, s32[8,128]{1,0:T(8,128)} %bitcast.20, bf16[6,1024]{1,0:T(8,128)(2,1)} %w1s_hbm.1, bf16[6,1024]{1,0:T(8,128)(2,1)} %w1n_hbm.1, ...), custom_call_target="tpu_custom_call" | custom-call | tf_op jit(solution)/shard_map/step/pallas_call | solution.py:484
  100.2 2.4 %finish.1 = (f32[1,1]{1,0:T(1,128)}, f32[6,1024]{1,0:T(8,128)}, f32[6,1024]{1,0:T(8,128)}, f32[8,128]{1,0:T(8,128)}, f32[153,1024]{1,0:T(8,128)}, /*index=5*/f32[153,1024]{1,0:T(8,128)}, f32[1,153]{1,0:T(1,128)}) custom-call(bf16[2,4,4,80,128]{4,3,2,1,0:T(8,128)(2,1)} %get-tuple-element.16.full, f32[8,16,128]{2,1,0:T(8,128)} %get-tuple-element.17.g1), custom_call_target="tpu_custom_call" | custom-call | tf_op jit(solution)/shard_map/finish/pallas_call | solution.py:500

commit v3 on v2

v3 whole, which is shorter than its diff:
```python
import jax
import jax.numpy as jnp
from jax import lax
from jax.experimental import pallas as pl
from jax.experimental.pallas import tpu as pltpu
from jax.sharding import PartitionSpec as P

f32, bf16 = jnp.float32, jnp.bfloat16
loss_scale = 64.0

NZ, NG, NY, NX = 16, 8, 4, 4
TARGETS = 8 * NZ * NG * NY
LOW = 512
HIGH = 65536 // LOW
COLS = 6
FAN = 25
CLASSES = 153
LOSS_LANE = 200
SPAN = 128
NP = NX * NY
NBR_AT = 159
TAIL_AT = 312
GRAD_ROWS = 384
PART = GRAD_ROWS // NY
BLOCK = PART // 4
NEAR = (0, 1, NZ - 1, 2)
VMEM = pltpu.VMEM

SEMS = {}
total_sems = 0
for stage, slots in (
    ("w_g", NG), ("aux", NG), ("w_far", 4), ("w_near", 4), ("x_z", NZ), ("x_g", NG), ("xg", NG), ("lr", NG), ("gl", NG),
    ("gp_far", 4), ("gp_near", 4), ("scatter", 16), ("far", 4), ("near", 4), ("plane", NP), ("core", NP),
    ("dw", NG), ("y2", NY),
):
    SEMS[stage] = total_sems
    total_sems += slots


def dot(a, b, ca=1, cb=0):
    return lax.dot_general(a, b, (((ca,), (cb,)), ((), ())), preferred_element_type=f32)


def iota(shape, dim):
    return lax.broadcasted_iota(jnp.int32, shape, dim)


def step_kernel(
    feat_hbm, self_hbm, nbr_hbm, counts_hbm, w1s_hbm, w1n_hbm, bias1_hbm, w2s_hbm, w2n_hbm, bias2_hbm, labels_hbm,
    top_hbm, top_counts_hbm, full, g1_out,
    feat, self_ids, nbr_ids, nbr_counts, w1s, w1n, bias1, w2s, w2n, bias2, labels, top_ids, top_counts,
    split, table, wt, w_src, w_mid, w_all, aux, rows_t, rows_m, xp, x_src, x_in, x_mid, x_all, xg,
    lp, lr, gl_src, gl_all, gp_all, g2, ra, rb, rc, dw_src, dw_in, y2, send_sem, recv_sem, load_sem,
):
    o = lax.axis_index("cols")
    y = lax.axis_index("rep")
    z = o // NG
    g = o % NG
    x = g // 2
    c = g % 2
    here = x * NY + y

    def to_z(p):
        return {"cols": ((z + p) % NZ) * NG + g, "rep": y}

    def to_g(p):
        return {"cols": z * NG + (g + p) % NG, "rep": y}

    def to_y(p):
        return {"cols": o, "rep": (y + p) % NY}

    def to_plane(p):
        q = (here + p) % NP
        return {"cols": z * NG + (q // NY) * 2 + c, "rep": q % NY}

    to_core = {"cols": z * NG + x * 2 + (1 - c), "rep": y}

    def copy(stage, p, src, dst, device):
        at = SEMS[stage] + p
        return pltpu.make_async_remote_copy(
            src_ref=src, dst_ref=dst, send_sem=send_sem.at[at], recv_sem=recv_sem.at[at], device_id=device
        )

    def each(n, body, first=1):
        def run(p, carry):
            body(p)
            return carry
        lax.fori_loop(first, n, run, 0)

    arrivals, departures = {}, []

    def launch(stage, n, device, src, dst, got):
        def begin(i):
            p = n // 2 + ((i + 1) // 2) * (2 * (i % 2) - 1)
            copy(stage, p, src(p), dst, device(p)).start()

        each(n - 1, begin, 0)
        arrivals[stage] = lambda: each(n, lambda p: copy(stage, p, src(p), got(p), device(p)).wait_recv())
        departures.append(lambda: each(n, lambda p: copy(stage, p, src(p), dst, device(p)).wait_send()))

    def launch_near(stage, src, dst, got):
        steps = list(enumerate(NEAR))[1:]
        for i, p in steps:
            copy(stage, i, src, dst, to_z(p)).start()

        def wait_near():
            for i, p in steps:
                copy(stage, i, src, got((z + NZ - p) % 4), to_z(p)).wait_recv()

        def sent_near():
            for i, p in steps:
                copy(stage, i, src, dst, to_z(p)).wait_send()

        arrivals[stage] = wait_near
        departures.append(sent_near)

    def arrive(stage):
        arrivals.pop(stage)()

    def depart():
        while departures:
            departures.pop(0)()

    def to_far(p):
        return to_z(4 * p)

    row, col = z % 4, z // 4

    def far_of(p):
        return (col + 4 - p) % 4

    def z_of(p):
        return (z + NZ - p) % NZ

    def g_of(p):
        return (g + NG - p) % NG

    def y_of(p):
        return (y + NY - p) % NY

    loads = [
        pltpu.make_async_copy(src, dst, load_sem.at[i])
        for i, (src, dst) in enumerate((
            (w1s_hbm, w1s), (w1n_hbm, w1n), (top_counts_hbm, top_counts), (labels_hbm, labels), (top_hbm, top_ids),
            (feat_hbm, feat), (self_hbm, self_ids), (counts_hbm, nbr_counts), (nbr_hbm, nbr_ids),
            (bias1_hbm, bias1), (bias2_hbm, bias2), (w2s_hbm, w2s), (w2n_hbm, w2n),
        ))
    ]
    for load in loads:
        load.start()
    waiting = list(range(13))

    def ready(first, last):
        for i in range(first, last):
            waiting.remove(i)
            loads[i].wait()

    barrier = pltpu.get_barrier_semaphore()
    each(NZ, lambda p: pl.semaphore_signal(barrier, inc=1, device_id=to_z(p)))
    each(NG, lambda p: pl.semaphore_signal(barrier, inc=1, device_id=to_g(p)))

    def signal_plane(p):
        device = {"cols": z * NG + (p // (NY - 1)) * 2 + c, "rep": (y + 1 + p % (NY - 1)) % NY}
        pl.semaphore_signal(barrier, inc=1, device_id=device)

    each(NX * (NY - 1), signal_plane, 0)
    for step in NEAR[1:] + (NZ - 2,):
        each(NY, lambda p, step=step: pl.semaphore_signal(
            barrier, inc=1, device_id={"cols": ((z + step) % NZ) * NG + g, "rep": (y + p) % NY}
        ))

    with jax.named_scope("prepare"):
        wt[...] = jnp.zeros_like(wt)
        ready(0, 5)
        wt[0:COLS, :] = w1s[...].astype(f32)
        wt[COLS:2 * COLS, :] = w1n[...].astype(f32)
        for d in range(NG):
            w_src[d] = wt[:, d * SPAN:(d + 1) * SPAN].astype(bf16)
        w_mid[g] = w_src[g]

        eye = iota((8, 8), 0) == iota((8, 8), 1)

        def column(ref):
            return jnp.sum(jnp.where(eye, jnp.broadcast_to(ref[...].astype(f32), (8, 8)), 0.0), axis=1, keepdims=True)

        count_col = column(top_counts)
        label_col = column(labels)
        picks = top_ids[...]
        live_top = iota(picks.shape, 1).astype(f32) < count_col
        lane = iota((8, SPAN), 1)
        mine = jnp.where(lane == 8, count_col, jnp.where(lane == 9, label_col, 0.0))
        for s in range(8):
            n_s = jnp.sum(jnp.where(live_top & (picks == s), 1.0, 0.0), axis=1, keepdims=True)
            mine = jnp.where(lane == s, n_s, mine)
        aux[g] = mine

    with jax.named_scope("table"):
        ready(5, 6)

        def split_high(h, carry):
            piece = feat[:, pl.ds(pl.multiple_of(h * LOW, LOW), LOW)].astype(f32)
            for q in range(LOW // SPAN):
                split[q, pl.ds(pl.multiple_of(h * 8, 8), COLS), :] = piece[:, q * SPAN:(q + 1) * SPAN]
            return carry

        lax.fori_loop(0, HIGH, split_high, 0, unroll=8)
        for k in range(COLS):
            for q in range(LOW // SPAN):
                table[k * HIGH:(k + 1) * HIGH, q * SPAN:(q + 1) * SPAN] = (
                    split[q, pl.ds(k, HIGH, stride=8), :].astype(bf16)
                )

    with jax.named_scope("lookup"):
        ready(6, 9)
        io_low = iota((256, SPAN), 0).astype(f32).astype(bf16)
        io_high = iota((HIGH, SPAN), 0)
        counts = nbr_counts[...]

        def look(ids, alive):
            low = jnp.bitwise_and(ids, LOW - 1).astype(f32)
            high = jnp.where(alive, jnp.right_shift(ids, LOW.bit_length() - 1), -1)

            def hot_rows(first, j):
                at = jnp.broadcast_to((low[j:j + 1, :] - first).astype(bf16), (256, SPAN))
                return jnp.where(io_low == at, jnp.bfloat16(1), jnp.bfloat16(0))

            hot = jnp.concatenate([
                jnp.concatenate([hot_rows(float(first), j) for j in range(8)], axis=1) for first in range(0, LOW, 256)
            ], axis=0)
            mask = jnp.concatenate([io_high == high[j:j + 1, :] for j in range(8)], axis=1)
            got = dot(table[...], hot)
            return tuple(
                jnp.sum(jnp.where(mask, got[k * HIGH:(k + 1) * HIGH], 0.0).reshape(HIGH // 8, 8, 8 * SPAN), axis=0)
                for k in range(COLS)
            )

        def add_nbr(k, sums):
            return tuple(a + b for a, b in zip(sums, look(nbr_ids[k], counts > k)))

        own = look(self_ids[...], counts > 0)
        pl.semaphore_wait(barrier, NZ - 1 + NG - 1 + NX * (NY - 1) + 4 * (NY - 1))
        launch("w_g", NG, to_g, lambda p: w_src.at[(g + p) % NG], w_mid.at[g], lambda p: w_mid.at[g_of(p)])
        launch("aux", NG, to_g, lambda p: aux.at[g], aux.at[g], lambda p: aux.at[g_of(p)])
        sums = tuple(jnp.zeros((8, 8 * SPAN), f32) for _ in range(COLS))
        sums = lax.fori_loop(0, 5, add_nbr, sums, unroll=5)
        arrive("w_g")
        w_all[row, col] = w_mid[...].reshape(SPAN, SPAN)
        w_mine = w_all.at[row, col]
        launch("w_far", 4, to_far, lambda p: w_mine, w_mine, lambda p: w_all.at[row, far_of(p)])
        sums = lax.fori_loop(5, 15, add_nbr, sums, unroll=5)
        arrive("w_far")
        launch_near("w_near", w_all.at[row], w_all.at[row], lambda r: w_all.at[r])
        sums = lax.fori_loop(15, FAN, add_nbr, sums, unroll=5)

    with jax.named_scope("rows"):
        rows_t[...] = jnp.zeros_like(rows_t)
        for j in range(8):
            cut = slice(j * SPAN, (j + 1) * SPAN)
            count = counts[j:j + 1, :].astype(f32)
            for k in range(COLS):
                rows_t[j, k:k + 1, :] = jnp.sum(own[k][:, cut], axis=0, keepdims=True)
                rows_t[j, COLS + k:COLS + k + 1, :] = jnp.sum(sums[k][:, cut], axis=0, keepdims=True) / count
            rows_t[j, 2 * COLS:2 * COLS + 1, :] = jnp.ones((1, SPAN), f32)
        for j in range(8):
            rows_m[pl.ds(j, SPAN, stride=8), :] = rows_t[j].T
        for t in range(8):
            xp[t] = rows_m[t * SPAN:(t + 1) * SPAN, :].T[0:16, :].astype(bf16)

        odd = z % 2
        half = iota((16, SPAN), 1) // 64
        for t in range(8):
            straight = xp[t].astype(f32)
            turned = pltpu.roll(straight, 64, 1)
            x_src[2 * t] = jnp.where(half == odd, jnp.where(odd == 0, straight, turned), 0.0).astype(bf16)
            x_src[2 * t + 1] = jnp.where(half == odd, jnp.where(odd == 1, straight, turned), 0.0).astype(bf16)
        launch("x_z", NZ, to_z, lambda p: x_src.at[(z + p) % NZ], x_in.at[z], lambda p: x_in.at[z_of(p)])
        x_in[z] = x_src[z]
        xg[g] = xp[...]

    with jax.named_scope("lists"):
        arrive("aux")
        lists = aux[...].reshape(64, SPAN)
        top_div = lists[:, 8:9]
        spread = (iota((SPAN, 64), 0) == iota((SPAN, 64), 1) % 8).astype(f32).astype(bf16)
        same = iota((64, 64), 0) // 8 == iota((64, 64), 1) // 8
        picked = jnp.where(same, dot(lists.astype(bf16), spread), 0.0).astype(bf16)
        ready(9, 13)

    with jax.named_scope("rows_to_z"):
        arrive("w_near")
        depart()
        arrive("x_z")
    for t in range(8):
        x_mid[t] = x_in[2 * t] + x_in[2 * t + 1]
    launch("x_g", NG, to_g, lambda p: x_mid, x_all.at[g], lambda p: x_all.at[g_of(p)])
    x_all[g] = x_mid[...]

    with jax.named_scope("rows_over_g"):
        arrive("x_g")

    with jax.named_scope("layers"):
        both = jnp.zeros((SPAN, 2 * SPAN), f32)
        for t in range(8):
            left = x_all[:, t].reshape(SPAN, SPAN)
            right = jnp.concatenate([w_all[(2 * t + i) % 4, (2 * t + i) // 4] for i in range(2)], axis=1)
            both = both + dot(left, right, 0, 0)
        pre = both[0:64, 0:SPAN] + both[64:SPAN, SPAN:] + bias1[pl.ds(g, 1), :]
        hidden = jnp.maximum(pre, 0.0).astype(bf16)
        top_mean = (dot(picked, hidden) / top_div).astype(bf16)
        span = pl.ds(pl.multiple_of(g * SPAN, SPAN), SPAN)
        w2s_g = w2s[:, span]
        w2n_g = w2n[:, span]
        part = dot(hidden, w2s_g, 1, 1) + dot(top_mean, w2n_g, 1, 1)
        lp[...] = jnp.zeros_like(lp)
        lp[:, :, 0:CLASSES] = part.reshape(NG, 8, CLASSES)
        launch("lr", NG, to_g, lambda p: lp.at[(g + p) % NG], lr.at[g], lambda p: lr.at[g_of(p)])
        lr[g] = lp[g]
    with jax.named_scope("logits_wait"):
        depart()
        arrive("lr")

    with jax.named_scope("softmax"):
        logits = jnp.sum(lr[...], axis=0)[:, 0:CLASSES] + bias2[...]
        exps = jnp.exp(logits)
        total = jnp.sum(exps, axis=1, keepdims=True)
        onehot = jnp.where(iota((8, CLASSES), 1).astype(f32) == label_col, 1.0, 0.0)
        row_loss = jnp.log(total) - jnp.sum(onehot * logits, axis=1, keepdims=True)
        grad = ((exps / total - onehot) * (loss_scale / TARGETS)).astype(bf16)
        gl_src[...] = jnp.where(iota((8, 2 * SPAN), 1) == LOSS_LANE, row_loss, 0.0)
        gl_src[:, 0:CLASSES] = grad.astype(f32)
        launch("gl", NG, to_g, lambda p: gl_src, gl_all.at[g], lambda p: gl_all.at[g_of(p)])
        gl_all[g] = gl_src[...]
        g2[...] = jnp.zeros_like(g2)
    with jax.named_scope("grad_logits_wait"):
        arrive("gl")

    with jax.named_scope("classifier_grads"):
        gl_rows = gl_all[...].reshape(64, 2 * SPAN)
        gl = gl_rows[:, 0:CLASSES].astype(bf16)
        g2[0:CLASSES, :] = dot(gl, hidden, 0, 0)
        g2[NBR_AT:NBR_AT + CLASSES, :] = dot(gl, top_mean, 0, 0)
        col_sums = jnp.sum(gl_rows, axis=0, keepdims=True)
        g2[TAIL_AT:TAIL_AT + 1, :] = col_sums[:, 0:SPAN]
        g2[TAIL_AT + 1:TAIL_AT + 2, :] = col_sums[:, SPAN:]

        def block(r, d):
            return g2.at[pl.ds(pl.multiple_of((d * 4 + r) * BLOCK, 8), BLOCK)]

        def scatter(act, wait=False):
            for i, p in enumerate(NEAR):
                def run(q, i=i, p=p):
                    device = {"cols": ((z + p) % NZ) * NG + g, "rep": (y + q) % NY}
                    got = ra.at[i, y_of(q)] if wait else ra.at[i, y]
                    act(copy("scatter", i * 4 + q, block((z + p) % 4, (y + q) % NY), got, device))

                each(NY, run, 0 if i else 1)

        scatter(lambda send: send.start())
        departures.append(lambda: scatter(lambda send: send.wait_send()))
        ra[0, y] = g2[pl.ds(pl.multiple_of((y * 4 + row) * BLOCK, 8), BLOCK), :]

    with jax.named_scope("back"):
        back_top = dot(gl, w2n_g) / top_div
        top_1 = back_top.astype(bf16)
        rest = back_top - top_1.astype(f32)
        top_2 = rest.astype(bf16)
        top_3 = (rest - top_2.astype(f32)).astype(bf16)
        back = dot(gl, w2s_g) + (dot(picked, top_1, 0, 0) + (dot(picked, top_2, 0, 0) + dot(picked, top_3, 0, 0)))
        grad_pre = jnp.where(pre > 0.0, back, 0.0).astype(bf16)
        gp_all[row, col] = grad_pre
        mine_gp = gp_all.at[row, col]
        launch("gp_far", 4, to_far, lambda p: mine_gp, mine_gp, lambda p: gp_all.at[row, far_of(p)])
        launch("xg", NG, to_g, lambda p: xp, xg.at[g], lambda p: xg.at[g_of(p)])

    with jax.named_scope("scatter"):
        scatter(lambda send: send.wait_recv(), wait=True)
        rb[col] = jnp.sum(ra[...].reshape(4 * NY, BLOCK, SPAN), axis=0)
        mine_rb = rb.at[col]
        launch("far", 4, to_far, lambda p: mine_rb, mine_rb, lambda p: rb.at[far_of(p)])

    with jax.named_scope("grad_pre_far"):
        arrive("gp_far")
        launch_near("gp_near", gp_all.at[row], gp_all.at[row], lambda r: gp_all.at[r])

    with jax.named_scope("far"):
        arrive("far")
        rc[row] = jnp.sum(rb[...], axis=0)
        launch_near("near", rc.at[row], rc.at[row], lambda r: rc.at[r])

    with jax.named_scope("grad_pre_near"):
        arrive("xg")
        arrive("gp_near")
    with jax.named_scope("layer_grads"):
        dw = jnp.zeros((SPAN, SPAN), f32)
        for t in range(8):
            pair = [gp_all[(2 * t + i) % 4, (2 * t + i) // 4] for i in range(2)]
            dw = dw + dot(xg[:, t].reshape(SPAN, SPAN), jnp.concatenate(pair, axis=0))
        dw_src[...] = dw.reshape(NG, 16, SPAN)
        launch("dw", NG, to_g, lambda p: dw_src.at[(g + p) % NG], dw_in.at[g], lambda p: dw_in.at[g_of(p)])
        dw_in[g] = dw_src[g]

    with jax.named_scope("gather_over_z"):
        arrive("near")
        earlier = departures[:]
        departures.clear()
        fin = rc[...].reshape(PART, SPAN)
        low_part = fin - fin.astype(bf16).astype(f32)
        low_part = jnp.concatenate([low_part[0:2], low_part[0:PART - 2]], axis=0)
        at = iota((PART, SPAN), 0) - (TAIL_AT - (NY - 1) * PART)
        is_low = (y == NY - 1) & (at >= 2) & (at < 4)
        full[c, x, y] = jnp.where(is_low, low_part, fin).astype(bf16)
        out_block = full.at[c, x, y]
        each(NP, lambda p: copy("plane", p, out_block, out_block, to_plane(p)).start())
        departures.append(lambda: each(NP, lambda p: copy("plane", p, out_block, out_block, to_plane(p)).wait_send()))
        copy("core", here, out_block, out_block, to_core).start()

    with jax.named_scope("layer_grads_wait"):
        arrive("dw")
        y2[y] = dw_in[...]
        launch("y2", NY, to_y, lambda p: y2.at[y], y2.at[y], lambda p: y2.at[y_of(p)])

    with jax.named_scope("gather_over_plane"):
        for wait in earlier:
            wait()

        def forward(p):
            q = (here + NP - p) % NP
            there = full.at[c, q // NY, q % NY]
            copy("plane", p, out_block, there, to_plane(p)).wait_recv()
            copy("core", q, there, there, to_core).start()

        each(NP, forward)
        departures.append(lambda: each(NP, lambda q: copy("core", q, out_block, out_block, to_core).wait_send(), 0))

    with jax.named_scope("layer_grads_over_rep"):
        arrive("y2")
        g1_out[...] = jnp.sum(y2[...], axis=0)

    with jax.named_scope("gather_over_core"):
        def from_core(q):
            there = full.at[1 - c, q // NY, q % NY]
            copy("core", q, there, there, to_core).wait_recv()

        each(NP, from_core, 0)

    with jax.named_scope("sends"):
        depart()


def finish_kernel(full, g1, *refs):
    outs, bufs, sem = refs[0:7], refs[7:14], refs[14]
    loss, g1s, g1n, gb1, g2s, g2n, gb2 = bufs
    for d in range(NG):
        cut = slice(d * SPAN, (d + 1) * SPAN)
        g1s[:, cut] = g1[d, 0:COLS]
        g1n[:, cut] = g1[d, COLS:2 * COLS]
        gb1[d:d + 1, :] = g1[d, 2 * COLS:2 * COLS + 1]
    rows = full[0, 0, NY - 1].astype(f32)
    at = TAIL_AT - (NY - 1) * PART
    tail = rows[at:at + 2] + rows[at + 2:at + 4]
    gb2[:, 0:SPAN] = tail[0:1]
    gb2[:, SPAN:CLASSES] = tail[1:2, 0:CLASSES - SPAN]
    loss[...] = tail[1:2, LOSS_LANE - SPAN:LOSS_LANE - SPAN + 1] / TARGETS
    stores = []

    def store(src, dst):
        stores.append(pltpu.make_async_copy(src, dst, sem.at[len(stores)]))
        stores[-1].start()

    for i in (0, 1, 2, 3, 6):
        store(bufs[i], outs[i])
    for d in range(NG):
        cut = slice(d * SPAN, (d + 1) * SPAN)
        flat = full[d % 2, d // 2].astype(f32).reshape(GRAD_ROWS, SPAN)
        g2s[:, cut] = flat[0:CLASSES]
        g2n[:, cut] = flat[NBR_AT:NBR_AT + CLASSES]
        store(g2s.at[:, cut], outs[4].at[:, cut])
        store(g2n.at[:, cut], outs[5].at[:, cut])
    for copied in stores:
        copied.wait()


def per_device(
    features, self_ids, nbr_ids, nbr_counts, w1_self, w1_nbr, bias1, w2_self, w2_nbr, bias2, labels, top_ids, top_counts
):
    hidden = bias1.shape[0]
    operands = (
        features.T, self_ids.T, jnp.transpose(nbr_ids, (2, 1, 0)), nbr_counts.T, w1_self, w1_nbr,
        bias1.reshape(NG, SPAN), w2_self.T, w2_nbr.T, bias2.reshape(1, CLASSES), labels.reshape(1, 8),
        top_ids, top_counts.reshape(1, 8),
    )
    scratch = [VMEM(a.shape, a.dtype) for a in operands] + [
        VMEM((LOW // SPAN, HIGH * 8, SPAN), f32),
        VMEM((HIGH * COLS, LOW), bf16),
        VMEM((16, hidden), f32),
        VMEM((NG, 16, SPAN), bf16),
        VMEM((NG, 16, SPAN), bf16),
        VMEM((4, 4, SPAN, SPAN), bf16),
        VMEM((NG, 8, SPAN), f32),
        VMEM((8, SPAN, SPAN), f32),
        VMEM((8 * SPAN, SPAN), f32),
        VMEM((8, 16, SPAN), bf16),
        VMEM((NZ, 16, SPAN), bf16),
        VMEM((NZ, 16, SPAN), bf16),
        VMEM((8, 16, SPAN), bf16),
        VMEM((NG, 8, 16, SPAN), bf16),
        VMEM((NG, 8, 16, SPAN), bf16),
        VMEM((NG, 8, 2 * SPAN), f32),
        VMEM((NG, 8, 2 * SPAN), f32),
        VMEM((8, 2 * SPAN), f32),
        VMEM((NG, 8, 2 * SPAN), f32),
        VMEM((4, 4, 64, SPAN), bf16),
        VMEM((GRAD_ROWS, SPAN), f32),
        VMEM((4, NY, BLOCK, SPAN), f32),
        VMEM((4, BLOCK, SPAN), f32),
        VMEM((4, BLOCK, SPAN), f32),
        VMEM((NG, 16, SPAN), f32),
        VMEM((NG, 16, SPAN), f32),
        VMEM((NY, NG, 16, SPAN), f32),
        pltpu.SemaphoreType.DMA((total_sems,)),
        pltpu.SemaphoreType.DMA((total_sems,)),
        pltpu.SemaphoreType.DMA((len(operands),)),
    ]
    full, g1 = pl.pallas_call(
        step_kernel,
        out_shape=[
            jax.ShapeDtypeStruct((2, NX, NY, PART, SPAN), bf16), jax.ShapeDtypeStruct((NG, 16, SPAN), f32),
        ],
        in_specs=[pl.BlockSpec(memory_space=pltpu.HBM)] * len(operands),
        out_specs=[pl.BlockSpec(memory_space=VMEM)] * 2,
        scratch_shapes=scratch,
        compiler_params=pltpu.CompilerParams(
            collective_id=0, has_side_effects=True, vmem_limit_bytes=60 * 2**20
        ),
        name="step",
    )(*operands)
    shapes = (
        (1, 1), (COLS, hidden), (COLS, hidden), (NG, SPAN), (CLASSES, hidden), (CLASSES, hidden), (1, CLASSES),
    )
    loss, g1s, g1n, gb1, g2s, g2n, gb2 = pl.pallas_call(
        finish_kernel,
        out_shape=[jax.ShapeDtypeStruct(s, f32) for s in shapes],
        in_specs=[pl.BlockSpec(memory_space=VMEM)] * 2,
        out_specs=[pl.BlockSpec(memory_space=pltpu.HBM)] * len(shapes),
        scratch_shapes=[VMEM(s, f32) for s in shapes] + [pltpu.SemaphoreType.DMA((5 + 2 * NG,))],
        name="finish",
    )(full, g1)
    return loss.reshape(()), g1s, g1n, gb1.reshape(hidden), g2s.T, g2n.T, gb2.reshape(CLASSES)


def solution(mesh):
    in_specs = (
        P(None, "cols"), P(None, "rep"), P(None, "rep", None), P(None, "rep"), P("cols", None), P("cols", None),
        P(), P(), P(), P(), P(("cols", "rep")), P(("cols", "rep"), None), P(("cols", "rep")),
    )
    out_specs = (P(), P("cols", None), P("cols", None), P(), P(), P(), P())
    return jax.shard_map(per_device, mesh=mesh, in_specs=in_specs, out_specs=out_specs, check_vma=False)
```

time: 103 us -> 95.8 us (0.930)
  Pallas kernels: 102 us -> 95 us
    pallas_call x1, Pallas kernels: 99.6 us -> 92.5 us  [per_device(): pl.pallas_call(step_kernel, out_shape=[jax.ShapeDtypeStruct((2, NX, NY, P...]
where the time goes in v3:
time: 95.8 us; the launch traced here: 95.6 us
  Pallas kernels  95 us (99%)
    pallas_call x1, Pallas kernels, per_device(): pl.pallas_call(step_kernel, out_shape=[jax.ShapeDtypeStruct((2, NX, NY, P...  92.5 us
    pallas_call x1, Pallas kernels, per_device(): pl.pallas_call(finish_kernel, out_shape=[jax.ShapeDtypeStruct(s, f32) for...  2.47 us

profile of v3, /device:TPU:1, one launch (start us, length us, event | category | flops | bytes accessed | tf_op | source)
XLA Modules:
  0.0 95.6 jit_solution(2114703451373868182)
XLA Ops:
  0.6 92.5 %step.1 = (bf16[2,4,4,96,128]{4,3,2,1,0:T(8,128)(2,1)}, f32[8,16,128]{2,1,0:T(8,128)}) custom-call(bf16[6,65536]{1,0:T(8,128)(2,1)} %bitcast.15, s32[8,128]{1,0:T(8,128)} %bitcast.19, s32[25,8,128]{2,1,0:T(8,128)} %bitcast.18, s32[8,128]{1,0:T(8,128)} %bitcast.20, bf16[6,1024]{1,0:T(8,128)(2,1)} %w1s_hbm.1, bf16[6,1024]{1,0:T(8,128)(2,1)} %w1n_hbm.1, ...), custom_call_target="tpu_custom_call" | custom-call | tf_op jit(solution)/shard_map/step/pallas_call | solution.py:524
  93.1 2.5 %finish.1 = (f32[1,1]{1,0:T(1,128)}, f32[6,1024]{1,0:T(8,128)}, f32[6,1024]{1,0:T(8,128)}, f32[8,128]{1,0:T(8,128)}, f32[153,1024]{1,0:T(8,128)}, /*index=5*/f32[153,1024]{1,0:T(8,128)}, f32[1,153]{1,0:T(1,128)}) custom-call(bf16[2,4,4,96,128]{4,3,2,1,0:T(8,128)(2,1)} %get-tuple-element.16.full, f32[8,16,128]{2,1,0:T(8,128)} %get-tuple-element.17.g1), custom_call_target="tpu_custom_call" | custom-call | tf_op jit(solution)/shard_map/finish/pallas_call | solution.py:540

commit v4 on v3

--- a/solution.py
+++ b/solution.py
@@ -50,7 +50,7 @@
     top_hbm, top_counts_hbm, full, g1_out,
     feat, self_ids, nbr_ids, nbr_counts, w1s, w1n, bias1, w2s, w2n, bias2, labels, top_ids, top_counts,
     split, table, wt, w_src, w_mid, w_all, aux, rows_t, rows_m, xp, x_src, x_in, x_mid, x_all, xg,
-    lp, lr, gl_src, gl_all, gp_all, g2, ra, rb, rc, dw_src, dw_in, y2, send_sem, recv_sem, load_sem,
+    lp, lr, gl_src, gl_all, gp_all, g2, ra, rb, rc, spread, dw_src, dw_in, y2, send_sem, recv_sem, load_sem, keep_sem,
 ):
     o = lax.axis_index("cols")
     y = lax.axis_index("rep")
@@ -141,8 +141,8 @@
     loads = [
         pltpu.make_async_copy(src, dst, load_sem.at[i])
         for i, (src, dst) in enumerate((
-            (w1s_hbm, w1s), (w1n_hbm, w1n), (top_counts_hbm, top_counts), (labels_hbm, labels), (top_hbm, top_ids),
-            (feat_hbm, feat), (self_hbm, self_ids), (counts_hbm, nbr_counts), (nbr_hbm, nbr_ids),
+            (feat_hbm, feat), (w1s_hbm, w1s), (w1n_hbm, w1n), (top_counts_hbm, top_counts), (labels_hbm, labels),
+            (top_hbm, top_ids), (self_hbm, self_ids), (counts_hbm, nbr_counts), (nbr_hbm, nbr_ids),
             (bias1_hbm, bias1), (bias2_hbm, bias2), (w2s_hbm, w2s), (w2n_hbm, w2n),
         ))
     ]
@@ -156,22 +156,24 @@
             loads[i].wait()
 
     barrier = pltpu.get_barrier_semaphore()
-    each(NZ, lambda p: pl.semaphore_signal(barrier, inc=1, device_id=to_z(p)))
-    each(NG, lambda p: pl.semaphore_signal(barrier, inc=1, device_id=to_g(p)))
-
-    def signal_plane(p):
-        device = {"cols": z * NG + (p // (NY - 1)) * 2 + c, "rep": (y + 1 + p % (NY - 1)) % NY}
-        pl.semaphore_signal(barrier, inc=1, device_id=device)
-
-    each(NX * (NY - 1), signal_plane, 0)
-    for step in NEAR[1:] + (NZ - 2,):
-        each(NY, lambda p, step=step: pl.semaphore_signal(
-            barrier, inc=1, device_id={"cols": ((z + step) % NZ) * NG + g, "rep": (y + p) % NY}
-        ))
+    others = [to_z(p) for p in sorted(range(1, NZ), key=lambda p: abs(p - NZ // 2))]
+    others += [
+        {"cols": ((z + step) % NZ) * NG + g, "rep": (y + p) % NY} for step in NEAR[1:] + (NZ - 2,) for p in range(1, NY)
+    ]
+    others += [{"cols": z * NG + i * 2 + c, "rep": (y + p) % NY} for i in range(NX) for p in range(1, NY)]
+    others += [to_g(p) for p in range(1, NG)]
+    n_others = len(others)
+
+    def greet(n):
+        for device in others[:n]:
+            pl.semaphore_signal(barrier, inc=1, device_id=device)
+        del others[:n]
+
+    greet(NZ - 1)
 
     with jax.named_scope("prepare"):
         wt[...] = jnp.zeros_like(wt)
-        ready(0, 5)
+        ready(1, 6)
         wt[0:COLS, :] = w1s[...].astype(f32)
         wt[COLS:2 * COLS, :] = w1n[...].astype(f32)
         for d in range(NG):
@@ -195,15 +197,15 @@
         aux[g] = mine
 
     with jax.named_scope("table"):
-        ready(5, 6)
-
-        def split_high(h, carry):
-            piece = feat[:, pl.ds(pl.multiple_of(h * LOW, LOW), LOW)].astype(f32)
+        ready(0, 1)
+
+        for h in range(HIGH):
+            piece = feat[:, h * LOW:(h + 1) * LOW].astype(f32)
             for q in range(LOW // SPAN):
-                split[q, pl.ds(pl.multiple_of(h * 8, 8), COLS), :] = piece[:, q * SPAN:(q + 1) * SPAN]
-            return carry
-
-        lax.fori_loop(0, HIGH, split_high, 0, unroll=8)
+                split[q, h * 8:h * 8 + COLS, :] = piece[:, q * SPAN:(q + 1) * SPAN]
+            if h % 3 == 2:
+                greet(1)
+        greet(len(others))
         for k in range(COLS):
             for q in range(LOW // SPAN):
                 table[k * HIGH:(k + 1) * HIGH, q * SPAN:(q + 1) * SPAN] = (
@@ -238,7 +240,7 @@
             return tuple(a + b for a, b in zip(sums, look(nbr_ids[k], counts > k)))
 
         own = look(self_ids[...], counts > 0)
-        pl.semaphore_wait(barrier, NZ - 1 + NG - 1 + NX * (NY - 1) + 4 * (NY - 1))
+        pl.semaphore_wait(barrier, n_others)
         launch("w_g", NG, to_g, lambda p: w_src.at[(g + p) % NG], w_mid.at[g], lambda p: w_mid.at[g_of(p)])
         launch("aux", NG, to_g, lambda p: aux.at[g], aux.at[g], lambda p: aux.at[g_of(p)])
         sums = tuple(jnp.zeros((8, 8 * SPAN), f32) for _ in range(COLS))
@@ -281,9 +283,9 @@
         arrive("aux")
         lists = aux[...].reshape(64, SPAN)
         top_div = lists[:, 8:9]
-        spread = (iota((SPAN, 64), 0) == iota((SPAN, 64), 1) % 8).astype(f32).astype(bf16)
+        repeat = (iota((SPAN, 64), 0) == iota((SPAN, 64), 1) % 8).astype(f32).astype(bf16)
         same = iota((64, 64), 0) // 8 == iota((64, 64), 1) // 8
-        picked = jnp.where(same, dot(lists.astype(bf16), spread), 0.0).astype(bf16)
+        picked = jnp.where(same, dot(lists.astype(bf16), repeat), 0.0).astype(bf16)
         ready(9, 13)
 
     with jax.named_scope("rows_to_z"):
@@ -408,15 +410,22 @@
         low_part = jnp.concatenate([low_part[0:2], low_part[0:PART - 2]], axis=0)
         at = iota((PART, SPAN), 0) - (TAIL_AT - (NY - 1) * PART)
         is_low = (y == NY - 1) & (at >= 2) & (at < 4)
-        full[c, x, y] = jnp.where(is_low, low_part, fin).astype(bf16)
-        out_block = full.at[c, x, y]
+        spread[x, y] = jnp.where(is_low, low_part, fin).astype(bf16)
+        out_block = spread.at[x, y]
         each(NP, lambda p: copy("plane", p, out_block, out_block, to_plane(p)).start())
-        departures.append(lambda: each(NP, lambda p: copy("plane", p, out_block, out_block, to_plane(p)).wait_send()))
-        copy("core", here, out_block, out_block, to_core).start()
+
+        def keep(q):
+            return pltpu.make_async_copy(spread.at[q // NY, q % NY], full.at[c, q // NY, q % NY], keep_sem.at[q])
+
+        def to_other_core(q):
+            return copy("core", q, spread.at[q // NY, q % NY], full.at[c, q // NY, q % NY], to_core)
+
+        keep(here).start()
+        to_other_core(here).start()
 
     with jax.named_scope("layer_grads_wait"):
         arrive("dw")
-        y2[y] = dw_in[...]
+        y2[y] = dw_in[...].astype(bf16)
         launch("y2", NY, to_y, lambda p: y2.at[y], y2.at[y], lambda p: y2.at[y_of(p)])
 
     with jax.named_scope("gather_over_plane"):
@@ -425,21 +434,22 @@
 
         def forward(p):
             q = (here + NP - p) % NP
-            there = full.at[c, q // NY, q % NY]
-            copy("plane", p, out_block, there, to_plane(p)).wait_recv()
-            copy("core", q, there, there, to_core).start()
+            copy("plane", p, out_block, spread.at[q // NY, q % NY], to_plane(p)).wait_recv()
+            to_other_core(q).start()
+            keep(q).start()
 
         each(NP, forward)
-        departures.append(lambda: each(NP, lambda q: copy("core", q, out_block, out_block, to_core).wait_send(), 0))
+        departures.append(lambda: each(NP, lambda p: copy("plane", p, out_block, out_block, to_plane(p)).wait_send()))
+        departures.append(lambda: each(NP, lambda q: to_other_core(q).wait_send(), 0))
+        departures.append(lambda: each(NP, lambda q: keep(q).wait(), 0))
 
     with jax.named_scope("layer_grads_over_rep"):
         arrive("y2")
-        g1_out[...] = jnp.sum(y2[...], axis=0)
+        g1_out[...] = jnp.sum(y2[...].astype(f32), axis=0)
 
     with jax.named_scope("gather_over_core"):
         def from_core(q):
-            there = full.at[1 - c, q // NY, q % NY]
-            copy("core", q, there, there, to_core).wait_recv()
+            copy("core", q, spread.at[q // NY, q % NY], full.at[1 - c, q // NY, q % NY], to_core).wait_recv()
 
         each(NP, from_core, 0)
 
@@ -447,14 +457,23 @@
         depart()
 
 
-def finish_kernel(full, g1, *refs):
-    outs, bufs, sem = refs[0:7], refs[7:14], refs[14]
+def finish_kernel(full_hbm, g1_hbm, *refs):
+    outs, bufs, full, g1, load_sem, sem = refs[0:7], refs[7:14], refs[14], refs[15], refs[16], refs[17]
     loss, g1s, g1n, gb1, g2s, g2n, gb2 = bufs
+    blocks = [
+        pltpu.make_async_copy(full_hbm.at[d % 2, d // 2], full.at[d % 2, d // 2], load_sem.at[d]) for d in range(NG)
+    ]
+    small = pltpu.make_async_copy(g1_hbm, g1, load_sem.at[NG])
+    small.start()
+    for block in blocks:
+        block.start()
+    small.wait()
     for d in range(NG):
         cut = slice(d * SPAN, (d + 1) * SPAN)
         g1s[:, cut] = g1[d, 0:COLS]
         g1n[:, cut] = g1[d, COLS:2 * COLS]
         gb1[d:d + 1, :] = g1[d, 2 * COLS:2 * COLS + 1]
+    blocks[0].wait()
     rows = full[0, 0, NY - 1].astype(f32)
     at = TAIL_AT - (NY - 1) * PART
     tail = rows[at:at + 2] + rows[at + 2:at + 4]
@@ -471,6 +490,8 @@
         store(bufs[i], outs[i])
     for d in range(NG):
         cut = slice(d * SPAN, (d + 1) * SPAN)
+        if d:
+            blocks[d].wait()
         flat = full[d % 2, d // 2].astype(f32).reshape(GRAD_ROWS, SPAN)
         g2s[:, cut] = flat[0:CLASSES]
         g2n[:, cut] = flat[NBR_AT:NBR_AT + CLASSES]
@@ -514,12 +535,14 @@
         VMEM((4, NY, BLOCK, SPAN), f32),
         VMEM((4, BLOCK, SPAN), f32),
         VMEM((4, BLOCK, SPAN), f32),
+        VMEM((NX, NY, PART, SPAN), bf16),
         VMEM((NG, 16, SPAN), f32),
         VMEM((NG, 16, SPAN), f32),
-        VMEM((NY, NG, 16, SPAN), f32),
+        VMEM((NY, NG, 16, SPAN), bf16),
         pltpu.SemaphoreType.DMA((total_sems,)),
         pltpu.SemaphoreType.DMA((total_sems,)),
         pltpu.SemaphoreType.DMA((len(operands),)),
+        pltpu.SemaphoreType.DMA((NP,)),
     ]
     full, g1 = pl.pallas_call(
         step_kernel,
@@ -527,7 +550,7 @@
             jax.ShapeDtypeStruct((2, NX, NY, PART, SPAN), bf16), jax.ShapeDtypeStruct((NG, 16, SPAN), f32),
         ],
         in_specs=[pl.BlockSpec(memory_space=pltpu.HBM)] * len(operands),
-        out_specs=[pl.BlockSpec(memory_space=VMEM)] * 2,
+        out_specs=[pl.BlockSpec(memory_space=pltpu.HBM), pl.BlockSpec(memory_space=VMEM)],
         scratch_shapes=scratch,
         compiler_params=pltpu.CompilerParams(
             collective_id=0, has_side_effects=True, vmem_limit_bytes=60 * 2**20
@@ -540,9 +563,13 @@
     loss, g1s, g1n, gb1, g2s, g2n, gb2 = pl.pallas_call(
         finish_kernel,
         out_shape=[jax.ShapeDtypeStruct(s, f32) for s in shapes],
-        in_specs=[pl.BlockSpec(memory_space=VMEM)] * 2,
+        in_specs=[pl.BlockSpec(memory_space=pltpu.HBM)] * 2,
         out_specs=[pl.BlockSpec(memory_space=pltpu.HBM)] * len(shapes),
-        scratch_shapes=[VMEM(s, f32) for s in shapes] + [pltpu.SemaphoreType.DMA((5 + 2 * NG,))],
+        scratch_shapes=[VMEM(s, f32) for s in shapes] + [
+            VMEM(full.shape, bf16), VMEM(g1.shape, f32),
+            pltpu.SemaphoreType.DMA((NG + 1,)), pltpu.SemaphoreType.DMA((5 + 2 * NG,)),
+        ],
+        compiler_params=pltpu.CompilerParams(vmem_limit_bytes=60 * 2**20),
         name="finish",
     )(full, g1)
     return loss.reshape(()), g1s, g1n, gb1.reshape(hidden), g2s.T, g2n.T, gb2.reshape(CLASSES)

time: 95.8 us -> 95.2 us (level)
  no operation moved by 1% of the time
where the time goes in v4:
time: 95.2 us; the launch traced here: 95 us
  Pallas kernels  94.4 us (99%)
    pallas_call x1, Pallas kernels, per_device(): pl.pallas_call(step_kernel, out_shape=[jax.ShapeDtypeStruct((2, NX, NY, P...  92 us
    pallas_call x1, Pallas kernels, per_device(): pl.pallas_call(finish_kernel, out_shape=[jax.ShapeDtypeStruct(s, f32) for...  2.34 us

profile of v4, /device:TPU:1, one launch (start us, length us, event | category | flops | bytes accessed | tf_op | source)
XLA Modules:
  0.0 95.0 jit_solution(16532924214763368612)
XLA Ops:
  0.6 92.0 %step.1 = (bf16[2,4,4,96,128]{4,3,2,1,0:T(8,128)(2,1)}, f32[8,16,128]{2,1,0:T(8,128)}) custom-call(bf16[6,65536]{1,0:T(8,128)(2,1)} %bitcast.15, s32[8,128]{1,0:T(8,128)} %bitcast.19, s32[25,8,128]{2,1,0:T(8,128)} %bitcast.18, s32[8,128]{1,0:T(8,128)} %bitcast.20, bf16[6,1024]{1,0:T(8,128)(2,1)} %w1s_hbm.1, bf16[6,1024]{1,0:T(8,128)(2,1)} %w1n_hbm.1, ...), custom_call_target="tpu_custom_call" | custom-call | tf_op jit(solution)/shard_map/step/pallas_call | solution.py:547
  92.7 2.3 %finish.1 = (f32[1,1]{1,0:T(1,128)}, f32[6,1024]{1,0:T(8,128)}, f32[6,1024]{1,0:T(8,128)}, f32[8,128]{1,0:T(8,128)}, f32[153,1024]{1,0:T(8,128)}, /*index=5*/f32[153,1024]{1,0:T(8,128)}, f32[1,153]{1,0:T(1,128)}) custom-call(bf16[2,4,4,96,128]{4,3,2,1,0:T(8,128)(2,1)} %get-tuple-element.16.full_hbm, f32[8,16,128]{2,1,0:T(8,128)} %get-tuple-element.17.g1_hbm), custom_call_target="tpu_custom_call" | custom-call | tf_op jit(solution)/shard_map/finish/pallas_call | solution.py:563

commit v5 on v4

--- a/solution.py
+++ b/solution.py
@@ -29,7 +29,7 @@
 SEMS = {}
 total_sems = 0
 for stage, slots in (
-    ("w_g", NG), ("aux", NG), ("w_far", 4), ("w_near", 4), ("x_z", NZ), ("x_g", NG), ("xg", NG), ("lr", NG), ("gl", NG),
+    ("w_g", NG), ("aux", NG), ("w_far", 4), ("w_near", 4), ("x_z", NZ), ("x_g0", NG), ("x_g1", NG), ("xg", NG), ("lr", NG), ("gl", NG),
     ("gp_far", 4), ("gp_near", 4), ("scatter", 16), ("far", 4), ("near", 4), ("plane", NP), ("core", NP),
     ("dw", NG), ("y2", NY),
 ):
@@ -231,10 +231,13 @@
             ], axis=0)
             mask = jnp.concatenate([io_high == high[j:j + 1, :] for j in range(8)], axis=1)
             got = dot(table[...], hot)
-            return tuple(
-                jnp.sum(jnp.where(mask, got[k * HIGH:(k + 1) * HIGH], 0.0).reshape(HIGH // 8, 8, 8 * SPAN), axis=0)
-                for k in range(COLS)
-            )
+            found = []
+            for k in range(COLS):
+                one = jnp.zeros((8, 8 * SPAN), f32)
+                for b in range(0, HIGH, 8):
+                    one = jnp.where(mask[b:b + 8], got[k * HIGH + b:k * HIGH + b + 8], one)
+                found.append(one)
+            return tuple(found)
 
         def add_nbr(k, sums):
             return tuple(a + b for a, b in zip(sums, look(nbr_ids[k], counts > k)))
@@ -287,24 +290,40 @@
         same = iota((64, 64), 0) // 8 == iota((64, 64), 1) // 8
         picked = jnp.where(same, dot(lists.astype(bf16), repeat), 0.0).astype(bf16)
         ready(9, 13)
+        lp[...] = jnp.zeros_like(lp)
 
     with jax.named_scope("rows_to_z"):
         arrive("w_near")
+        arrivals.pop("x_z")
+        pairs = [(z // 2 + p) % 8 for p in (0, 1, 7, 2, 6, 3, 5, 4)]
+
+        def z_pair(i):
+            for odd_z in range(2):
+                if i == 0 and odd_z:
+                    continue
+                source = 2 * pairs[i] + odd_z if i else 2 * pairs[0] + 1 - odd
+                copy("x_z", (z + NZ - source) % NZ, x_src.at[0], x_in.at[source], to_z(1)).wait_recv()
+            x_mid[i // 4, i % 4] = x_in[2 * pairs[i]] + x_in[2 * pairs[i] + 1]
+
+        for half_z in range(2):
+            for i in range(4):
+                z_pair(4 * half_z + i)
+            launch(
+                f"x_g{half_z}", NG, to_g, lambda p, h=half_z: x_mid.at[h], x_all.at[g, half_z],
+                lambda p, h=half_z: x_all.at[g_of(p), h],
+            )
+        x_all[g] = x_mid[...]
+
+    with jax.named_scope("rows_over_g"):
         depart()
-        arrive("x_z")
-    for t in range(8):
-        x_mid[t] = x_in[2 * t] + x_in[2 * t + 1]
-    launch("x_g", NG, to_g, lambda p: x_mid, x_all.at[g], lambda p: x_all.at[g_of(p)])
-    x_all[g] = x_mid[...]
-
-    with jax.named_scope("rows_over_g"):
-        arrive("x_g")
-
+        arrive("x_g0")
+        arrive("x_g1")
     with jax.named_scope("layers"):
         both = jnp.zeros((SPAN, 2 * SPAN), f32)
         for t in range(8):
-            left = x_all[:, t].reshape(SPAN, SPAN)
-            right = jnp.concatenate([w_all[(2 * t + i) % 4, (2 * t + i) // 4] for i in range(2)], axis=1)
+            left = x_all[:, t // 4, t % 4].reshape(SPAN, SPAN)
+            sources = [2 * pairs[t] + i for i in range(2)]
+            right = jnp.concatenate([w_all[source % 4, source // 4] for source in sources], axis=1)
             both = both + dot(left, right, 0, 0)
         pre = both[0:64, 0:SPAN] + both[64:SPAN, SPAN:] + bias1[pl.ds(g, 1), :]
         hidden = jnp.maximum(pre, 0.0).astype(bf16)
@@ -313,7 +332,6 @@
         w2s_g = w2s[:, span]
         w2n_g = w2n[:, span]
         part = dot(hidden, w2s_g, 1, 1) + dot(top_mean, w2n_g, 1, 1)
-        lp[...] = jnp.zeros_like(lp)
         lp[:, :, 0:CLASSES] = part.reshape(NG, 8, CLASSES)
         launch("lr", NG, to_g, lambda p: lp.at[(g + p) % NG], lr.at[g], lambda p: lr.at[g_of(p)])
         lr[g] = lp[g]
@@ -389,18 +407,6 @@
         rc[row] = jnp.sum(rb[...], axis=0)
         launch_near("near", rc.at[row], rc.at[row], lambda r: rc.at[r])
 
-    with jax.named_scope("grad_pre_near"):
-        arrive("xg")
-        arrive("gp_near")
-    with jax.named_scope("layer_grads"):
-        dw = jnp.zeros((SPAN, SPAN), f32)
-        for t in range(8):
-            pair = [gp_all[(2 * t + i) % 4, (2 * t + i) // 4] for i in range(2)]
-            dw = dw + dot(xg[:, t].reshape(SPAN, SPAN), jnp.concatenate(pair, axis=0))
-        dw_src[...] = dw.reshape(NG, 16, SPAN)
-        launch("dw", NG, to_g, lambda p: dw_src.at[(g + p) % NG], dw_in.at[g], lambda p: dw_in.at[g_of(p)])
-        dw_in[g] = dw_src[g]
-
     with jax.named_scope("gather_over_z"):
         arrive("near")
         earlier = departures[:]
@@ -422,6 +428,18 @@
 
         keep(here).start()
         to_other_core(here).start()
+
+    with jax.named_scope("grad_pre_near"):
+        arrive("xg")
+        arrive("gp_near")
+    with jax.named_scope("layer_grads"):
+        dw = jnp.zeros((SPAN, SPAN), f32)
+        for t in range(8):
+            pair = [gp_all[(2 * t + i) % 4, (2 * t + i) // 4] for i in range(2)]
+            dw = dw + dot(xg[:, t].reshape(SPAN, SPAN), jnp.concatenate(pair, axis=0))
+        dw_src[...] = dw.reshape(NG, 16, SPAN)
+        launch("dw", NG, to_g, lambda p: dw_src.at[(g + p) % NG], dw_in.at[g], lambda p: dw_in.at[g_of(p)])
+        dw_in[g] = dw_src[g]
 
     with jax.named_scope("layer_grads_wait"):
         arrive("dw")
@@ -523,8 +541,8 @@
         VMEM((8, 16, SPAN), bf16),
         VMEM((NZ, 16, SPAN), bf16),
         VMEM((NZ, 16, SPAN), bf16),
-        VMEM((8, 16, SPAN), bf16),
-        VMEM((NG, 8, 16, SPAN), bf16),
+        VMEM((2, 4, 16, SPAN), bf16),
+        VMEM((NG, 2, 4, 16, SPAN), bf16),
         VMEM((NG, 8, 16, SPAN), bf16),
         VMEM((NG, 8, 2 * SPAN), f32),
         VMEM((NG, 8, 2 * SPAN), f32),

time: 95.2 us -> 93.8 us (0.985)
  Pallas kernels: 94.4 us -> 92.9 us
    pallas_call x1, Pallas kernels: 92 us -> 90.6 us  [per_device(): pl.pallas_call(step_kernel, out_shape=[jax.ShapeDtypeStruct((2, NX, NY, P...]
where the time goes in v5:
time: 93.8 us; the launch traced here: 93.6 us
  Pallas kernels  92.9 us (99%)
    pallas_call x1, Pallas kernels, per_device(): pl.pallas_call(step_kernel, out_shape=[jax.ShapeDtypeStruct((2, NX, NY, P...  90.6 us
    pallas_call x1, Pallas kernels, per_device(): pl.pallas_call(finish_kernel, out_shape=[jax.ShapeDtypeStruct(s, f32) for...  2.34 us

profile of v5, /device:TPU:1, one launch (start us, length us, event | category | flops | bytes accessed | tf_op | source)
XLA Modules:
  0.0 93.6 jit_solution(1996367638870761933)
XLA Ops:
  0.6 90.6 %step.1 = (bf16[2,4,4,96,128]{4,3,2,1,0:T(8,128)(2,1)}, f32[8,16,128]{2,1,0:T(8,128)}) custom-call(bf16[6,65536]{1,0:T(8,128)(2,1)} %bitcast.15, s32[8,128]{1,0:T(8,128)} %bitcast.19, s32[25,8,128]{2,1,0:T(8,128)} %bitcast.18, s32[8,128]{1,0:T(8,128)} %bitcast.20, bf16[6,1024]{1,0:T(8,128)(2,1)} %w1s_hbm.1, bf16[6,1024]{1,0:T(8,128)(2,1)} %w1n_hbm.1, ...), custom_call_target="tpu_custom_call" | custom-call | tf_op jit(solution)/shard_map/step/pallas_call | solution.py:565
  91.2 2.3 %finish.1 = (f32[1,1]{1,0:T(1,128)}, f32[6,1024]{1,0:T(8,128)}, f32[6,1024]{1,0:T(8,128)}, f32[8,128]{1,0:T(8,128)}, f32[153,1024]{1,0:T(8,128)}, /*index=5*/f32[153,1024]{1,0:T(8,128)}, f32[1,153]{1,0:T(1,128)}) custom-call(bf16[2,4,4,96,128]{4,3,2,1,0:T(8,128)(2,1)} %get-tuple-element.16.full_hbm, f32[8,16,128]{2,1,0:T(8,128)} %get-tuple-element.17.g1_hbm), custom_call_target="tpu_custom_call" | custom-call | tf_op jit(solution)/shard_map/finish/pallas_call | solution.py:581

commit v6 on v5

--- a/solution.py
+++ b/solution.py
@@ -70,8 +70,15 @@
         return {"cols": o, "rep": (y + p) % NY}
 
     def to_plane(p):
-        q = (here + p) % NP
-        return {"cols": z * NG + (q // NY) * 2 + c, "rep": q % NY}
+        return {"cols": z * NG + ((x + p // NY) % NX) * 2 + c, "rep": (y + p % NY) % NY}
+
+    def plane_of(p):
+        return (x + NX - p // NY) % NX, (y + NY - p % NY) % NY
+
+    def ring(step, n):
+        return min(step % n, -step % n)
+
+    plane_steps = sorted(range(1, NP), key=lambda p: -(ring(p // NY, NX) + ring(p % NY, NY)))
 
     to_core = {"cols": z * NG + x * 2 + (1 - c), "rep": y}
 
@@ -90,12 +97,14 @@
     arrivals, departures = {}, []
 
     def launch(stage, n, device, src, dst, got):
-        def begin(i):
-            p = n // 2 + ((i + 1) // 2) * (2 * (i % 2) - 1)
+        for p in sorted(range(1, n), key=lambda p: abs(p - n // 2)):
             copy(stage, p, src(p), dst, device(p)).start()
 
-        each(n - 1, begin, 0)
-        arrivals[stage] = lambda: each(n, lambda p: copy(stage, p, src(p), got(p), device(p)).wait_recv())
+        def wait_all():
+            for p in range(1, n):
+                copy(stage, p, src(p), got(p), device(p)).wait_recv()
+
+        arrivals[stage] = wait_all
         departures.append(lambda: each(n, lambda p: copy(stage, p, src(p), dst, device(p)).wait_send()))
 
     def launch_near(stage, src, dst, got):
@@ -367,13 +376,11 @@
             return g2.at[pl.ds(pl.multiple_of((d * 4 + r) * BLOCK, 8), BLOCK)]
 
         def scatter(act, wait=False):
-            for i, p in enumerate(NEAR):
-                def run(q, i=i, p=p):
-                    device = {"cols": ((z + p) % NZ) * NG + g, "rep": (y + q) % NY}
-                    got = ra.at[i, y_of(q)] if wait else ra.at[i, y]
-                    act(copy("scatter", i * 4 + q, block((z + p) % 4, (y + q) % NY), got, device))
-
-                each(NY, run, 0 if i else 1)
+            steps = [(i, q) for i in range(4) for q in range(NY) if i or q]
+            for i, q in sorted(steps, key=lambda iq: -(ring(NEAR[iq[0]], NZ) + ring(iq[1], NY))):
+                device = {"cols": ((z + NEAR[i]) % NZ) * NG + g, "rep": (y + q) % NY}
+                got = ra.at[i, y_of(q)] if wait else ra.at[i, y]
+                act(copy("scatter", i * 4 + q, block((z + NEAR[i]) % 4, (y + q) % NY), got, device))
 
         scatter(lambda send: send.start())
         departures.append(lambda: scatter(lambda send: send.wait_send()))
@@ -418,7 +425,8 @@
         is_low = (y == NY - 1) & (at >= 2) & (at < 4)
         spread[x, y] = jnp.where(is_low, low_part, fin).astype(bf16)
         out_block = spread.at[x, y]
-        each(NP, lambda p: copy("plane", p, out_block, out_block, to_plane(p)).start())
+        for p in plane_steps:
+            copy("plane", p, out_block, out_block, to_plane(p)).start()
 
         def keep(q):
             return pltpu.make_async_copy(spread.at[q // NY, q % NY], full.at[c, q // NY, q % NY], keep_sem.at[q])
@@ -450,18 +458,18 @@
         for wait in earlier:
             wait()
 
-        def forward(p):
-            q = (here + NP - p) % NP
-            copy("plane", p, out_block, spread.at[q // NY, q % NY], to_plane(p)).wait_recv()
-            to_other_core(q).start()
-            keep(q).start()
-
-        each(NP, forward)
+        for p in plane_steps:
+            x_from, y_from = plane_of(p)
+            copy("plane", p, out_block, spread.at[x_from, y_from], to_plane(p)).wait_recv()
+            to_other_core(x_from * NY + y_from).start()
+            keep(x_from * NY + y_from).start()
+
         departures.append(lambda: each(NP, lambda p: copy("plane", p, out_block, out_block, to_plane(p)).wait_send()))
         departures.append(lambda: each(NP, lambda q: to_other_core(q).wait_send(), 0))
         departures.append(lambda: each(NP, lambda q: keep(q).wait(), 0))
 
     with jax.named_scope("layer_grads_over_rep"):
+        depart()
         arrive("y2")
         g1_out[...] = jnp.sum(y2[...].astype(f32), axis=0)
 
@@ -470,9 +478,6 @@
             copy("core", q, spread.at[q // NY, q % NY], full.at[1 - c, q // NY, q % NY], to_core).wait_recv()
 
         each(NP, from_core, 0)
-
-    with jax.named_scope("sends"):
-        depart()
 
 
 def finish_kernel(full_hbm, g1_hbm, *refs):

time: 93.8 us -> 94.1 us (level)
  no operation moved by 1% of the time
where the time goes in v6:
time: 94.1 us; the launch traced here: 93.9 us
  Pallas kernels  93.1 us (99%)
    pallas_call x1, Pallas kernels, per_device(): pl.pallas_call(step_kernel, out_shape=[jax.ShapeDtypeStruct((2, NX, NY, P...  90.8 us
    pallas_call x1, Pallas kernels, per_device(): pl.pallas_call(finish_kernel, out_shape=[jax.ShapeDtypeStruct(s, f32) for...  2.34 us

profile of v6, /device:TPU:1, one launch (start us, length us, event | category | flops | bytes accessed | tf_op | source)
XLA Modules:
  0.0 93.9 jit_solution(11961354935597262375)
XLA Ops:
  0.6 90.8 %step.1 = (bf16[2,4,4,96,128]{4,3,2,1,0:T(8,128)(2,1)}, f32[8,16,128]{2,1,0:T(8,128)}) custom-call(bf16[6,65536]{1,0:T(8,128)(2,1)} %bitcast.15, s32[8,128]{1,0:T(8,128)} %bitcast.19, s32[25,8,128]{2,1,0:T(8,128)} %bitcast.18, s32[8,128]{1,0:T(8,128)} %bitcast.20, bf16[6,1024]{1,0:T(8,128)(2,1)} %w1s_hbm.1, bf16[6,1024]{1,0:T(8,128)(2,1)} %w1n_hbm.1, ...), custom_call_target="tpu_custom_call" | custom-call | tf_op jit(solution)/shard_map/step/pallas_call | solution.py:570
  91.4 2.3 %finish.1 = (f32[1,1]{1,0:T(1,128)}, f32[6,1024]{1,0:T(8,128)}, f32[6,1024]{1,0:T(8,128)}, f32[8,128]{1,0:T(8,128)}, f32[153,1024]{1,0:T(8,128)}, /*index=5*/f32[153,1024]{1,0:T(8,128)}, f32[1,153]{1,0:T(1,128)}) custom-call(bf16[2,4,4,96,128]{4,3,2,1,0:T(8,128)(2,1)} %get-tuple-element.16.full_hbm, f32[8,16,128]{2,1,0:T(8,128)} %get-tuple-element.17.g1_hbm), custom_call_target="tpu_custom_call" | custom-call | tf_op jit(solution)/shard_map/finish/pallas_call | solution.py:586
